TPU v7x, 256 devices: a whole 4x4x8 slice. The times are simulated.
256 devices in a mesh: dom: 64 (over x, z, core), sub: 4 (over y).
Axes of the slice: x: 4, y: 4, z: 8, core: 2. Of those that a mesh axis runs over, the one named last changes fastest.
Arguments:
- positions: float32 [3, 2097152], P(None, ('dom', 'sub')), may hold values from 0 to 1
- masses: float32 [2097152], P(('dom', 'sub')), may hold values from 0.00029296876 to 0.0029296875
- cell_mass: float32 [32768], P(('dom', 'sub')), may hold values from 0.00234375 to 0.0234375
- cell_center: float32 [3, 32768], P(None, ('dom', 'sub')), may hold values from 0 to 1
- cell_quad: float32 [6, 32768], P(None, ('dom', 'sub')), may hold values from -0.0046875 to 0.0046875
- cell_list: int32 [32768, 128], P(('dom', 'sub')), may hold values from 0 to 32767
- leaf_list: int32 [32768, 16], P(('dom', 'sub')), may hold values from 0 to 575, as said below
- send_list: int32 [64, 4, 8, 8], P('dom', 'sub'), may hold values from 0 to 127
- send_count: int32 [64, 4, 8], P('dom', 'sub'), may hold values from 1 to 8, as said below
Outputs:
- accel: float32 [3, 2097152], P(None, ('dom', 'sub'))
Inputs may be any that keep to these rules, and one draw needn't show every extreme that they name: `send_count`: counts fall off with the distance along the curve: an offset of one domain always carries 8 blocks, an offset of d domains at most max(1, 8 // d). `leaf_list`: each id names a block of the group's own domain or a slot of the far part that carries a block.
All inputs are finite; a program needn't handle non-finite values.
Results may differ from a plain program's by a relative error of at most 0.0003.
Values sent between devices are 32-bit elements; how exact they have to be, the bound alone decides.
A program may use at most 128 MiB of HBM per device.

v0:
```python
import jax
import jax.numpy as jnp
from jax import lax
from jax.sharding import PartitionSpec as P

LEAF = 64
LEAF_DEV = 128
NCELL = 128
NLEAF = 16
RANGE = 4
CAP = 8


softening_sq = 0.0025


def passed_along(value, axis, steps):
    count = lax.axis_size(axis)
    leading, last = (max(0, -steps), min(count, count - steps))
    return lax.ppermute(value, axis, [(source, source + steps) for source in range(leading, last)])


def direct_pull(targets, sources, weights):
    offset = sources[:, :, None, :] - targets[:, :, :, None]
    dist_sq = jnp.sum(offset * offset, axis=0) + softening_sq
    factor = weights[:, None, :] / (dist_sq * jnp.sqrt(dist_sq))
    return jnp.sum(offset * factor[None], axis=-1)


def multipole_pull(targets, moments):
    offset = targets[:, :, :, None] - moments[1:4, :, None, :]
    dist_sq = jnp.sum(offset * offset, axis=0) + softening_sq
    inv_one = 1.0 / jnp.sqrt(dist_sq)
    inv_two = inv_one * inv_one
    inv_three = inv_one * inv_two
    inv_five = inv_three * inv_two
    inv_seven = inv_five * inv_two
    quad_part = moments[4:10, :, None, :]
    q_times_x = quad_part[0] * offset[0] + quad_part[3] * offset[1] + quad_part[4] * offset[2]
    q_times_y = quad_part[3] * offset[0] + quad_part[1] * offset[1] + quad_part[5] * offset[2]
    q_times_z = quad_part[4] * offset[0] + quad_part[5] * offset[1] + quad_part[2] * offset[2]
    q_times = jnp.stack([q_times_x, q_times_y, q_times_z])
    quad_form = jnp.sum(offset * q_times, axis=0)
    mass_part = moments[0, :, None, :]
    accel_terms = (
        -mass_part * inv_three * offset + inv_five * q_times - 2.5 * inv_seven * quad_form * offset
    )
    return jnp.sum(accel_terms, axis=-1)


def group_pull(targets, essential, leaf_ids, cell_table, cell_ids):
    groups_here = leaf_ids.shape[0]
    particle_ids = (
        leaf_ids[:, :, None] * LEAF + jnp.arange(LEAF, dtype=jnp.int32)[None, None, :]
    ).reshape(groups_here, -1)
    picked = essential[:, particle_ids]
    moments = cell_table[:, cell_ids]
    return direct_pull(targets, picked[0:3], picked[3]) + multipole_pull(targets, moments)


def on_device(
    positions,
    masses,
    cell_mass,
    cell_center,
    cell_quad,
    cell_list,
    leaf_list,
    send_list,
    send_count,
):
    offset_values = list(range(-RANGE, 0)) + list(range(1, RANGE + 1))
    cell_table = jnp.concatenate([cell_mass[None], cell_center, cell_quad], axis=0)
    all_cells = lax.all_gather(cell_table, ("dom", "sub"), axis=1, tiled=True)
    packed = jnp.concatenate([positions, masses[None]], axis=0)
    nearby = lax.all_gather(packed, "sub", axis=1, tiled=True)
    chosen = send_list.reshape(2 * RANGE, CAP)
    counts = send_count.reshape(2 * RANGE)
    live = (jnp.arange(CAP, dtype=jnp.int32)[None, :] < counts[:, None]).astype(jnp.float32)
    weight = jnp.repeat(live.reshape(-1), LEAF).reshape(2 * RANGE, CAP * LEAF)
    flat_ids = (
        chosen[:, :, None] * LEAF + jnp.arange(LEAF, dtype=jnp.int32)[None, None, :]
    ).reshape(2 * RANGE, CAP * LEAF)
    outgoing = packed[:, flat_ids] * weight[None]
    pieces = []
    for slot in range(2 * RANGE):
        pieces.append(passed_along(outgoing[:, slot], "dom", offset_values[slot]))
    remote = jnp.stack(pieces, axis=1)
    essential = jnp.concatenate([nearby, remote.reshape(4, 2 * RANGE * CAP * LEAF)], axis=1)
    block_size = 8
    block_count = LEAF_DEV // block_size
    target_blocks = positions.reshape(3, block_count, block_size, LEAF).transpose(1, 0, 2, 3)
    leaf_blocks = leaf_list.reshape(block_count, block_size, NLEAF)
    cell_blocks = cell_list.reshape(block_count, block_size, NCELL)

    def one_block(inputs):
        block_targets, block_leaves, block_cells = inputs
        return group_pull(block_targets, essential, block_leaves, all_cells, block_cells)

    pulled = lax.map(one_block, (target_blocks, leaf_blocks, cell_blocks))
    return pulled.transpose(1, 0, 2, 3).reshape(3, LEAF_DEV * LEAF)


def solution(mesh):
    return jax.shard_map(
        on_device,
        mesh=mesh,
        in_specs=(
            P(None, ("dom", "sub")),
            P(("dom", "sub")),
            P(("dom", "sub")),
            P(None, ("dom", "sub")),
            P(None, ("dom", "sub")),
            P(("dom", "sub"), None),
            P(("dom", "sub"), None),
            P("dom", "sub", None, None),
            P("dom", "sub", None),
        ),
        out_specs=P(None, ("dom", "sub")),
        check_vma=False,
    )
```

profile of v0, /device:TPU:1, one launch (start us, length us, event | category | flops | bytes accessed | tf_op | source)
XLA Modules:
  0.0 975.4 jit_solution(4220310291080115131)
XLA Ops:
  6.6 1.0 pad_maximum_fusion.2
  7.6 2.6 copy.47
  10.5 12.9 %gather_fusion.2 = f32[4096,4]{1,0:T(8,128)S(1)} fusion(f32[4,8192]{0,1:T(8,128)} %copy.47, s32[4096]{0:T(1024)S(1)} %broadcast_clamp_fusion), kind=kCustom, calls=%fused_computation.2 | custom fusion | bytes 147456 | tf_op jit(solution)/shard_map/gather | solution.py:84
  24.4 1.3 collective-permute-start
  25.7 1.3 collective-permute-start.1
  27.0 1.3 collective-permute-start.2
  28.3 5.1 collective-permute-start.3
  33.5 4.2 collective-permute-start.4
  38.3 4.3 collective-permute-start.5
  42.7 4.1 collective-permute-start.6
  46.8 5.3 collective-permute-start.7
  52.1 10.8 %all_gather.6 = f32[4,32768]{1,0:T(4,128)S(1)} all-gather(f32[4,8192]{1,0:T(4,128)S(1)} %pad_maximum_fusion.2), channel_id=1, replica_groups=mesh['dom'=64,'sub'=4] {'sub'}, dimensions={1}, use_global_device_ids=true | all-gather | bytes 655360 | tf_op jit(solution)/shard_map/all_gather | solution.py:76
  63.7 9.8 %copy.56 = f32[4,36864]{0,1:T(8,128)} copy(f32[4,36864]{1,0:T(4,128)S(1)} %pad_maximum_fusion.1) | data formatting | bytes 1179648 | tf_op jit(solution)/shard_map/while | solution.py:100
  73.5 75.3 %all-gather.2.cloned.1.call-done = f32[10,32768]{1,0:T(8,128)} async-done(((f32[10,128]{1,0:T(8,128)}), f32[10,32768]{1,0:T(8,128)}) %all-gather.2.cloned.1.call-update) | async-done | bytes 1310736 | tf_op jit(solution)/shard_map/all_gather | solution.py:74
  148.8 9.7 copy.58
  158.5 809.3 %while.10 = (s32[]{:T(128)}, f32[16,3,8,64]{3,2,1,0:T(8,128)S(1)}, s32[16,8,16]{2,1,0:T(8,128)S(1)}, f32[4,36864]{0,1:T(8,128)}, f32[16,3,8,64]{3,2,0,1:T(8,128)...) while((s32[]{:T(128)}, f32[16,3,8,64]{3,2,1,0:T(8,128)S(1)}, s32[16,8,16]{2,1,0:T(8,128)S(1)}, ...), condition=%wide.region_6.7_spmd, body=%wide.region_0.6_spmd.sunk | while | flops 15249026 | bytes 16653933 | solution.py:100
  158.8 34.1 %gather_fusion = f32[8192,4]{1,0:T(8,128)} fusion(f32[4,36864]{0,1:T(8,128)} %get-tuple-element.193, s32[8192]{0:T(1024)S(1)} %bitcast_clamp_fusion.2), kind=kCustom, calls=%fused_computation.clone.1 | custom fusion | bytes 294912 | tf_op jit(solution)/shard_map/while/body/eval_jaxpr/gather | solution.py:56
  192.9 2.9 copy.69
  198.8 8.6 gather_fusion.1
  209.4 34.1 %gather_fusion = f32[8192,4]{1,0:T(8,128)} fusion(f32[4,36864]{0,1:T(8,128)} %get-tuple-element.193, s32[8192]{0:T(1024)S(1)} %bitcast_clamp_fusion.2), kind=kCustom, calls=%fused_computation.clone.1 | custom fusion | bytes 294912 | tf_op jit(solution)/shard_map/while/body/eval_jaxpr/gather | solution.py:56
  243.5 2.9 copy.69
  249.4 8.6 gather_fusion.1
  259.9 34.1 %gather_fusion = f32[8192,4]{1,0:T(8,128)} fusion(f32[4,36864]{0,1:T(8,128)} %get-tuple-element.193, s32[8192]{0:T(1024)S(1)} %bitcast_clamp_fusion.2), kind=kCustom, calls=%fused_computation.clone.1 | custom fusion | bytes 294912 | tf_op jit(solution)/shard_map/while/body/eval_jaxpr/gather | solution.py:56
  294.1 2.9 copy.69
  300.0 8.6 gather_fusion.1
  310.5 34.1 %gather_fusion = f32[8192,4]{1,0:T(8,128)} fusion(f32[4,36864]{0,1:T(8,128)} %get-tuple-element.193, s32[8192]{0:T(1024)S(1)} %bitcast_clamp_fusion.2), kind=kCustom, calls=%fused_computation.clone.1 | custom fusion | bytes 294912 | tf_op jit(solution)/shard_map/while/body/eval_jaxpr/gather | solution.py:56
  344.7 2.9 copy.69
  350.6 8.6 gather_fusion.1
  361.1 34.1 %gather_fusion = f32[8192,4]{1,0:T(8,128)} fusion(f32[4,36864]{0,1:T(8,128)} %get-tuple-element.193, s32[8192]{0:T(1024)S(1)} %bitcast_clamp_fusion.2), kind=kCustom, calls=%fused_computation.clone.1 | custom fusion | bytes 294912 | tf_op jit(solution)/shard_map/while/body/eval_jaxpr/gather | solution.py:56
  395.2 2.9 copy.69
  401.2 8.6 gather_fusion.1
  411.7 34.1 %gather_fusion = f32[8192,4]{1,0:T(8,128)} fusion(f32[4,36864]{0,1:T(8,128)} %get-tuple-element.193, s32[8192]{0:T(1024)S(1)} %bitcast_clamp_fusion.2), kind=kCustom, calls=%fused_computation.clone.1 | custom fusion | bytes 294912 | tf_op jit(solution)/shard_map/while/body/eval_jaxpr/gather | solution.py:56
  445.8 2.9 copy.69
  451.7 8.6 gather_fusion.1
  462.3 34.1 %gather_fusion = f32[8192,4]{1,0:T(8,128)} fusion(f32[4,36864]{0,1:T(8,128)} %get-tuple-element.193, s32[8192]{0:T(1024)S(1)} %bitcast_clamp_fusion.2), kind=kCustom, calls=%fused_computation.clone.1 | custom fusion | bytes 294912 | tf_op jit(solution)/shard_map/while/body/eval_jaxpr/gather | solution.py:56
  496.4 2.9 copy.69
  502.3 8.6 gather_fusion.1
  512.8 34.1 %gather_fusion = f32[8192,4]{1,0:T(8,128)} fusion(f32[4,36864]{0,1:T(8,128)} %get-tuple-element.193, s32[8192]{0:T(1024)S(1)} %bitcast_clamp_fusion.2), kind=kCustom, calls=%fused_computation.clone.1 | custom fusion | bytes 294912 | tf_op jit(solution)/shard_map/while/body/eval_jaxpr/gather | solution.py:56
  547.0 2.9 copy.69
  552.9 8.6 gather_fusion.1
  563.4 34.1 %gather_fusion = f32[8192,4]{1,0:T(8,128)} fusion(f32[4,36864]{0,1:T(8,128)} %get-tuple-element.193, s32[8192]{0:T(1024)S(1)} %bitcast_clamp_fusion.2), kind=kCustom, calls=%fused_computation.clone.1 | custom fusion | bytes 294912 | tf_op jit(solution)/shard_map/while/body/eval_jaxpr/gather | solution.py:56
  597.6 2.9 copy.69
  603.5 8.6 gather_fusion.1
  614.0 34.1 %gather_fusion = f32[8192,4]{1,0:T(8,128)} fusion(f32[4,36864]{0,1:T(8,128)} %get-tuple-element.193, s32[8192]{0:T(1024)S(1)} %bitcast_clamp_fusion.2), kind=kCustom, calls=%fused_computation.clone.1 | custom fusion | bytes 294912 | tf_op jit(solution)/shard_map/while/body/eval_jaxpr/gather | solution.py:56
  648.2 2.9 copy.69
  654.1 8.6 gather_fusion.1
  664.6 34.1 %gather_fusion = f32[8192,4]{1,0:T(8,128)} fusion(f32[4,36864]{0,1:T(8,128)} %get-tuple-element.193, s32[8192]{0:T(1024)S(1)} %bitcast_clamp_fusion.2), kind=kCustom, calls=%fused_computation.clone.1 | custom fusion | bytes 294912 | tf_op jit(solution)/shard_map/while/body/eval_jaxpr/gather | solution.py:56
  698.7 2.9 copy.69
  704.6 8.6 gather_fusion.1
  715.2 34.1 %gather_fusion = f32[8192,4]{1,0:T(8,128)} fusion(f32[4,36864]{0,1:T(8,128)} %get-tuple-element.193, s32[8192]{0:T(1024)S(1)} %bitcast_clamp_fusion.2), kind=kCustom, calls=%fused_computation.clone.1 | custom fusion | bytes 294912 | tf_op jit(solution)/shard_map/while/body/eval_jaxpr/gather | solution.py:56
  749.3 2.9 copy.69
  755.2 8.6 gather_fusion.1
  765.8 34.1 %gather_fusion = f32[8192,4]{1,0:T(8,128)} fusion(f32[4,36864]{0,1:T(8,128)} %get-tuple-element.193, s32[8192]{0:T(1024)S(1)} %bitcast_clamp_fusion.2), kind=kCustom, calls=%fused_computation.clone.1 | custom fusion | bytes 294912 | tf_op jit(solution)/shard_map/while/body/eval_jaxpr/gather | solution.py:56
  799.9 2.9 copy.69
  805.8 8.6 gather_fusion.1
  816.3 34.1 %gather_fusion = f32[8192,4]{1,0:T(8,128)} fusion(f32[4,36864]{0,1:T(8,128)} %get-tuple-element.193, s32[8192]{0:T(1024)S(1)} %bitcast_clamp_fusion.2), kind=kCustom, calls=%fused_computation.clone.1 | custom fusion | bytes 294912 | tf_op jit(solution)/shard_map/while/body/eval_jaxpr/gather | solution.py:56
  850.5 2.9 copy.69
  856.4 8.6 gather_fusion.1
  866.9 34.1 %gather_fusion = f32[8192,4]{1,0:T(8,128)} fusion(f32[4,36864]{0,1:T(8,128)} %get-tuple-element.193, s32[8192]{0:T(1024)S(1)} %bitcast_clamp_fusion.2), kind=kCustom, calls=%fused_computation.clone.1 | custom fusion | bytes 294912 | tf_op jit(solution)/shard_map/while/body/eval_jaxpr/gather | solution.py:56
  901.1 2.9 copy.69
  907.0 8.6 gather_fusion.1
  917.5 34.1 %gather_fusion = f32[8192,4]{1,0:T(8,128)} fusion(f32[4,36864]{0,1:T(8,128)} %get-tuple-element.193, s32[8192]{0:T(1024)S(1)} %bitcast_clamp_fusion.2), kind=kCustom, calls=%fused_computation.clone.1 | custom fusion | bytes 294912 | tf_op jit(solution)/shard_map/while/body/eval_jaxpr/gather | solution.py:56
  951.6 2.9 copy.69
  957.6 8.6 gather_fusion.1
  (423 shorter events, 81.0 us)
Async XLA Ops:
  6.5 3.7 copy-start.2
  6.5 17.6 %copy-start.5 = (s32[1,1,8]{2,1,0:T(1,128)S(1)}, s32[1,1,8]{2,1,0:T(1,128)}, u32[]{:S(2)}) copy-start(s32[1,1,8]{2,1,0:T(1,128)} %param.19) | copy-start | bytes 100
  6.5 31.1 %copy-start.3 = (f32[6,128]{1,0:T(8,128)S(1)}, f32[6,128]{1,0:T(8,128)}, u32[]{:S(2)}) copy-start(f32[6,128]{1,0:T(8,128)} %param.15) | copy-start | bytes 9220
  6.5 31.1 %copy-start.4 = (f32[3,128]{1,0:T(4,128)S(1)}, f32[3,128]{1,0:T(4,128)}, u32[]{:S(2)}) copy-start(f32[3,128]{1,0:T(4,128)} %param.14) | copy-start | bytes 4612
  6.5 31.1 %copy-start.6 = (f32[128]{0:T(128)S(1)}, f32[128]{0:T(128)}, u32[]{:S(2)}) copy-start(f32[128]{0:T(128)} %param.13) | copy-start | bytes 1540
  6.5 142.3 %all-gather.2.cloned.1.call-start = ((), (), s32[]{:S(2)}) async-start(), calls=%async_computation | async-start | bytes 2105344 | tf_op jit(solution)/shard_map/all_gather | solution.py:74
  7.6 55.3 %copy-start = (f32[3,8192]{1,0:T(4,128)S(1)}, f32[3,8192]{1,0:T(4,128)}, u32[]{:S(2)}) copy-start(f32[3,8192]{1,0:T(4,128)} %param.11) | copy-start | bytes 294916
  7.6 55.5 %copy-start.1 = (s32[128,16]{0,1:T(8,128)S(1)}, s32[128,16]{0,1:T(8,128)}, u32[]{:S(2)}) copy-start(s32[128,16]{0,1:T(8,128)} %param.17) | copy-start | bytes 24580
  24.4 13.9 %collective-permute-start = (f32[4,512]{1,0:T(4,128)S(1)}, f32[4,512]{1,0:T(4,128)S(1)}, u32[]{:S(2)}, u32[]{:S(2)}) collective-permute-start(f32[4,512]{1,0:T(4,128)S(1)} %get-tuple-element.100), channel_id=1, source_target_pairs={{16,0},{20,4},{24,8},{28,12},{32,16},{36,20},{40,24},{44,28},{48,3... | collective-permute-start | bytes 24584 | tf_op jit(solution)/shard_map/ppermute | solution.py:20
  25.7 17.0 %collective-permute-start.1 = (f32[4,512]{1,0:T(4,128)S(1)}, f32[4,512]{1,0:T(4,128)S(1)}, u32[]{:S(2)}, u32[]{:S(2)}) collective-permute-start(f32[4,512]{1,0:T(4,128)S(1)} %get-tuple-element.99), channel_id=1, source_target_pairs={{12,0},{16,4},{20,8},{24,12},{28,16},{32,20},{36,24},{40,28},{44,3... | collective-permute-start | bytes 24584 | tf_op jit(solution)/shard_map/ppermute | solution.py:20
  27.0 19.8 %collective-permute-start.2 = (f32[4,512]{1,0:T(4,128)S(1)}, f32[4,512]{1,0:T(4,128)S(1)}, u32[]{:S(2)}, u32[]{:S(2)}) collective-permute-start(f32[4,512]{1,0:T(4,128)S(1)} %get-tuple-element.98), channel_id=1, source_target_pairs={{8,0},{12,4},{16,8},{20,12},{24,16},{28,20},{32,24},{36,28},{40,32... | collective-permute-start | bytes 24584 | tf_op jit(solution)/shard_map/ppermute | solution.py:20
  28.3 34.9 %collective-permute-start.3 = (f32[4,512]{1,0:T(4,128)S(1)}, f32[4,512]{1,0:T(4,128)S(1)}, u32[]{:S(2)}, u32[]{:S(2)}) collective-permute-start(f32[4,512]{1,0:T(4,128)S(1)} %get-tuple-element.97), channel_id=1, source_target_pairs={{4,0},{8,4},{12,8},{16,12},{20,16},{24,20},{28,24},{32,28},{36,32}... | collective-permute-start | bytes 24584 | tf_op jit(solution)/shard_map/ppermute | solution.py:20
  33.5 29.8 %collective-permute-start.4 = (f32[4,512]{1,0:T(4,128)S(1)}, f32[4,512]{1,0:T(4,128)S(1)}, u32[]{:S(2)}, u32[]{:S(2)}) collective-permute-start(f32[4,512]{1,0:T(4,128)S(1)} %get-tuple-element.96), channel_id=1, source_target_pairs={{0,4},{4,8},{8,12},{12,16},{16,20},{20,24},{24,28},{28,32},{32,36}... | collective-permute-start | bytes 24584 | tf_op jit(solution)/shard_map/ppermute | solution.py:20
  38.3 25.0 %collective-permute-start.5 = (f32[4,512]{1,0:T(4,128)S(1)}, f32[4,512]{1,0:T(4,128)S(1)}, u32[]{:S(2)}, u32[]{:S(2)}) collective-permute-start(f32[4,512]{1,0:T(4,128)S(1)} %get-tuple-element.95), channel_id=1, source_target_pairs={{0,8},{4,12},{8,16},{12,20},{16,24},{20,28},{24,32},{28,36},{32,40... | collective-permute-start | bytes 24584 | tf_op jit(solution)/shard_map/ppermute | solution.py:20
  42.7 20.7 %collective-permute-start.6 = (f32[4,512]{1,0:T(4,128)S(1)}, f32[4,512]{1,0:T(4,128)S(1)}, u32[]{:S(2)}, u32[]{:S(2)}) collective-permute-start(f32[4,512]{1,0:T(4,128)S(1)} %get-tuple-element.94), channel_id=1, source_target_pairs={{0,12},{4,16},{8,20},{12,24},{16,28},{20,32},{24,36},{28,40},{32,4... | collective-permute-start | bytes 24584 | tf_op jit(solution)/shard_map/ppermute | solution.py:20
  46.8 16.5 %collective-permute-start.7 = (f32[4,512]{1,0:T(4,128)S(1)}, f32[4,512]{1,0:T(4,128)S(1)}, u32[]{:S(2)}, u32[]{:S(2)}) collective-permute-start(f32[4,512]{1,0:T(4,128)S(1)} %get-tuple-element.93), channel_id=1, source_target_pairs={{0,16},{4,20},{8,24},{12,28},{16,32},{20,36},{24,40},{28,44},{32,4... | collective-permute-start | bytes 24584 | tf_op jit(solution)/shard_map/ppermute | solution.py:20
Sparse Core Ops, SparseCore 0:
  38.4 110.3 all-gather.1
where the time goes:
time: 978 us; the launch traced here: 975 us
  local copies, waits for them, and re-layouts  774 us (79%)
  waiting for transfers between devices  75.3 us (8%)
  other arithmetic  72.5 us (7%)
  starting transfers between devices  27 us (3%)
  between operations  13.7 us (1%)
  blocking collectives  10.8 us (1%)
    gather x32, local copies, waits for them, and re-layouts, group_pull(): picked = essential[:, particle_ids]  592 us
    gather x32, local copies, waits for them, and re-layouts, group_pull(): moments = cell_table[:, cell_ids]  140 us
    all_gather x1, waiting for transfers between devices, on_device(): all_cells = lax.all_gather(cell_table, ('dom', 'sub'), axis=1, tiled=True)  75.3 us
    ppermute x8, starting transfers between devices, passed_along(): lax.ppermute(value, axis, [(source, source + steps) for source in range(l...  27 us
  transfers between devices with their start and end apart: 9, of which 1 were waited for; matrix products, arithmetic and copies ran while one was open for 1% of the time, Pallas kernels for 0%

commit v1 on v0

v1 whole, which is shorter than its diff:
```python
import functools

import jax
import jax.numpy as jnp
from jax import lax
from jax.experimental import pallas as pl
from jax.experimental.pallas import tpu as pltpu
from jax.sharding import PartitionSpec as P

LEAF = 64
NCELL = 128
NLEAF = 16
RANGE = 4
CAP = 8
EPS = 0.0025
F32 = jnp.float32
BF16 = jnp.bfloat16
MESH = pl.DeviceIdType.MESH

NX, NY, NZ, NCORE = 4, 4, 8, 2
SIZES = {"x": NX, "y": NY, "z": NZ}
ROWS = 16
PARTS = ((0, 6, ("z", "x", "y")), (6, 5, ("x", "y", "z")), (11, 5, ("y", "z", "x")))
OFFSETS = tuple(range(-RANGE, 0)) + tuple(range(1, RANGE + 1))
PAIRS = 64
ALL_PAIRS = NY * PAIRS + len(OFFSETS) * CAP // 2
N_CELL_ROWS = NX * NY * NZ * NCORE * ROWS


def exchange_kernel(
    pos_ref, mass_ref, cmass_ref, ccen_ref, cquad_ref, send_list, send_count,
    leaf_ref, table_ref,
    pad, own, far_out, near_send, near_recv, far_send, far_recv, cell_send, cell_recv, core_send, core_recv,
):
    dom = lax.axis_index("dom")
    sub = lax.axis_index("sub")
    core = dom % NCORE
    at = {"x": dom // (NZ * NCORE), "z": (dom // NCORE) % NZ, "y": sub}

    def device(x, y, z, c):
        return ((x * NZ + z) * NCORE + c, y)

    def peer(axis, step):
        where = dict(at)
        where[axis] = (at[axis] + step) % SIZES[axis]
        return device(where["x"], where["y"], where["z"], core)

    barrier = pltpu.get_barrier_semaphore()
    waits = 0
    for axis in ("x", "y", "z"):
        for step in range(1, SIZES[axis]):
            pl.semaphore_signal(barrier, inc=1, device_id=peer(axis, step), device_id_type=MESH)
            waits += 1
    other_core = device(at["x"], at["y"], at["z"], 1 - core)
    pl.semaphore_signal(barrier, inc=1, device_id=other_core, device_id_type=MESH)
    waits += 1
    n_dom = NX * NZ * NCORE
    for off in OFFSETS:
        pl.semaphore_signal(barrier, inc=1, device_id=((dom + off + n_dom) % n_dom, sub), device_id_type=MESH)
        waits += 1

    base = sub * PAIRS
    for j in range(PAIRS):
        own[j, 0:3, :] = pos_ref[:, j * 128:(j + 1) * 128]
        own[j, 3:4, :] = mass_ref[j:j + 1, :]
    leaf_ref[pl.ds(base, PAIRS)] = own[...]
    pad[...] = jnp.zeros((128, 128), F32)
    pad[0:1, :] = cmass_ref[...]
    pad[1:4, :] = ccen_ref[...]
    pad[4:10, :] = cquad_ref[...]
    by_cell = pad[...].T
    packed = by_cell[0:16, :]
    for g in range(1, 8):
        packed = packed + pltpu.roll(by_cell[16 * g:16 * g + 16, :], 16 * g, 1)
    pad[0:16, :] = packed

    def start_of(part, done):
        first, rows, order = PARTS[part]
        size = rows
        n = N_CELL_ROWS // ROWS
        index = 0
        stride = 1
        for s, axis in enumerate(order):
            if s >= done:
                index = index + at[axis] * stride
            stride = stride * SIZES[axis]
        if done <= 3:
            index = index + core * stride
        for axis in order[:done]:
            size = size * SIZES[axis]
        return n * first + index * rows, size

    for part, (first, rows, order) in enumerate(PARTS):
        start, _ = start_of(part, 0)
        for r in range(rows):
            table_ref[start + r, :, :] = pad[first + r:first + r + 1, :]

    pl.semaphore_wait(barrier, waits)

    def cell_copy(part, stage, step):
        axis = PARTS[part][2][stage]
        start, size = start_of(part, stage)
        block = table_ref.at[pl.ds(start, size)]
        return pltpu.make_async_remote_copy(
            src_ref=block, dst_ref=block,
            send_sem=cell_send.at[part, stage, step], recv_sem=cell_recv.at[part, stage, step],
            device_id=peer(axis, step), device_id_type=MESH)

    def stage_copies(part, stage):
        return [cell_copy(part, stage, step) for step in range(1, SIZES[PARTS[part][2][stage]])]

    def core_copy(part):
        start, size = start_of(part, 3)
        block = table_ref.at[pl.ds(start, size)]
        return pltpu.make_async_remote_copy(
            src_ref=block, dst_ref=block, send_sem=core_send.at[part], recv_sem=core_recv.at[part],
            device_id=other_core, device_id_type=MESH)

    copies = [[stage_copies(part, stage) for stage in range(3)] for part in range(3)]
    core_copies = [core_copy(part) for part in range(3)]
    for part in range(3):
        for copy in copies[part][0]:
            copy.start()

    near = [
        pltpu.make_async_remote_copy(
            src_ref=own, dst_ref=leaf_ref.at[pl.ds(base, PAIRS)], send_sem=near_send.at[step], recv_sem=near_recv.at[step],
            device_id=peer("y", step), device_id_type=MESH)
        for step in range(1, NY)
    ]
    for copy in near:
        copy.start()

    low_half = lax.broadcasted_iota(jnp.int32, (4, 128), 1) < LEAF

    def far_pair(slot, t):
        halves = []
        for h in range(2):
            block = send_list[slot, 2 * t + h]
            tile = own[block // 2]
            turned = pltpu.roll(tile, LEAF, 1)
            picked = jnp.where(block % 2 == h, tile, turned)
            inside = jnp.logical_and(dom + OFFSETS[slot] >= 0, dom + OFFSETS[slot] < n_dom)
            live = jnp.logical_and(inside, 2 * t + h < send_count[slot])
            halves.append(jnp.where(live, picked, jnp.zeros_like(picked)))
        far_out[slot, t] = jnp.where(low_half, halves[0], halves[1])

    for slot in range(len(OFFSETS)):
        for t in range(CAP // 2):
            far_pair(slot, t)

    def far_copy(slot):
        return pltpu.make_async_remote_copy(
            src_ref=far_out.at[slot],
            dst_ref=leaf_ref.at[pl.ds(NY * PAIRS + slot * (CAP // 2), CAP // 2)],
            send_sem=far_send.at[slot], recv_sem=far_recv.at[slot],
            device_id=((dom + OFFSETS[slot] + n_dom) % n_dom, sub), device_id_type=MESH)

    far = [far_copy(slot) for slot in range(len(OFFSETS))]
    for copy in far:
        copy.start()

    for stage in range(3):
        for part in range(3):
            for copy in copies[part][stage]:
                copy.wait_recv()
            if stage < 2:
                for copy in copies[part][stage + 1]:
                    copy.start()
            else:
                core_copies[part].start()
    for copy in near:
        copy.wait()
    for copy in far:
        copy.wait()
    for part in range(3):
        for stage in range(3):
            for copy in copies[part][stage]:
                copy.wait_send()
        core_copies[part].wait()


def exchange(positions, masses, cell_mass, cell_center, cell_quad, send_list, send_count):
    vmem = pl.BlockSpec(memory_space=pltpu.VMEM)
    smem = pl.BlockSpec(memory_space=pltpu.SMEM)
    dma = pltpu.SemaphoreType.DMA
    return pl.pallas_call(
        exchange_kernel,
        name="exchange",
        out_shape=(
            jax.ShapeDtypeStruct((ALL_PAIRS, 4, 128), F32),
            jax.ShapeDtypeStruct((N_CELL_ROWS, 1, 128), F32),
        ),
        in_specs=[vmem] * 5 + [smem] * 2,
        out_specs=(vmem, vmem),
        scratch_shapes=[
            pltpu.VMEM((128, 128), F32),
            pltpu.VMEM((PAIRS, 4, 128), F32),
            pltpu.VMEM((len(OFFSETS), CAP // 2, 4, 128), F32),
            dma((NY,)), dma((NY,)), dma((len(OFFSETS),)), dma((len(OFFSETS),)),
            dma((3, 3, NZ)), dma((3, 3, NZ)), dma((3,)), dma((3,)),
        ],
        compiler_params=pltpu.CompilerParams(
            collective_id=0, has_side_effects=True, vmem_limit_bytes=24 * 1024 * 1024),
    )(positions, masses, cell_mass, cell_center, cell_quad, send_list, send_count)


def split3(value):
    high = value.astype(BF16).astype(F32)
    rest = value - high
    mid = rest.astype(BF16).astype(F32)
    return high, mid, rest - mid


def split2(value):
    high = value.astype(BF16)
    return high, (value - high.astype(F32)).astype(BF16)


def nt(a, b):
    return lax.dot_general(a, b, (((1,), (1,)), ((), ())), preferred_element_type=F32)


def cell_row(cell):
    shard = cell // 128
    sub = shard % NY
    dom = shard // NY
    at = {"x": dom // (NZ * NCORE), "z": (dom // NCORE) % NZ, "y": sub}
    core = dom % NCORE
    row = cell % 16
    n = N_CELL_ROWS // ROWS
    result = None
    for first, rows, order in PARTS:
        index, stride = 0, 1
        for axis in order:
            index = index + at[axis] * stride
            stride = stride * SIZES[axis]
        index = index + core * stride
        here = n * first + index * rows + (row - first)
        result = here if result is None else jnp.where(row >= first, here, result)
    return result


def pull_kernel(
    pos_ref, cells_ref, leaf_ids, leaf_ref, table_ref, out_ref,
    sources, targets, columns, rows_vmem, rows_smem, picked, row_sem,
):
    rows_vmem[...] = cell_row(cells_ref[...])
    row_copy = pltpu.make_async_copy(rows_vmem, rows_smem, row_sem)
    row_copy.start()

    row8 = lax.broadcasted_iota(jnp.int32, (8, 128), 0)
    one_row = jnp.where(row8 == 4, 1.0, 0.0).astype(F32)

    def prepare(pair, _):
        raw4 = leaf_ref[pair]
        raw = jnp.concatenate([raw4, raw4], axis=0)
        mass = raw4[3:4, :]
        centred = raw - 0.5
        square = jnp.where(row8 < 3, centred * centred, 0.0)
        norm = jnp.sum(square, axis=0, keepdims=True) + EPS
        u = jnp.where(row8 < 3, centred, jnp.where(row8 == 3, norm, one_row))
        s = jnp.where(row8 < 3, centred * mass, jnp.where(row8 == 3, mass, 0.0))
        u_high, u_mid, u_low = split3(u)
        s_high, s_mid, s_low = split3(s)
        s_top = s_high + pltpu.roll(s_mid, 4, 0)
        full = jnp.concatenate([u_high, u_mid, u_high, u_low, s_top, s_low], axis=0)
        sources[2 * pair] = full.astype(BF16)
        sources[2 * pair + 1] = pltpu.roll(full, LEAF, 1).astype(BF16)
        return 0

    lax.fori_loop(0, ALL_PAIRS, prepare, 0, unroll=4)

    for pair in range(PAIRS):
        raw3 = pos_ref[:, pair * 128:(pair + 1) * 128]
        raw = jnp.concatenate([raw3, jnp.zeros((5, 128), F32)], axis=0)
        centred = raw - 0.5
        square = jnp.where(row8 < 3, centred * centred, 0.0)
        norm = jnp.sum(square, axis=0, keepdims=True)
        t = jnp.where(row8 < 3, -2.0 * centred,
                      jnp.where(row8 == 3, 1.0, jnp.where(row8 == 4, norm, 0.0)))
        t_high, t_mid, t_low = split3(t)
        full = jnp.concatenate(
            [t_high, t_high, t_mid, t_mid, t_low, t_high, raw, jnp.zeros((128 - 56, 128), F32)], axis=0)
        turned = full.T
        targets[pair] = turned[:, 0:48].astype(BF16)
        columns[pair] = turned[:, 48:56]

    row_copy.wait()

    low_half = lax.broadcasted_iota(jnp.int32, (48, 128), 1) < LEAF
    summing_row = lax.broadcasted_iota(jnp.int32, (8, 768), 0)
    summing_lane = lax.broadcasted_iota(jnp.int32, (8, 768), 1)
    summing = jnp.where(summing_row == (summing_lane // 256), 1.0, 0.0).astype(BF16)

    def one_pair(pair, _):
        results = []
        centre = pos_ref[:, pl.ds(pl.multiple_of(pair * 128, 128), 128)] - 0.5
        for half in range(2):
            group = 2 * pair + half
            for k in range(NCELL):
                picked[half, k:k + 1, :] = table_ref[rows_smem[group, k]]
            lhs = targets[pair, half * 64:half * 64 + 64, :]
            total = None
            for tile in range(4):
                parts = []
                for j in range(2):
                    slot = 4 * tile + 2 * j
                    low = leaf_ids[slot, group]
                    high = leaf_ids[slot + 1, group]
                    parts.append(jnp.where(low_half, sources[low], sources[high ^ 1]))
                both = jnp.concatenate(parts, axis=1)
                rhs = jnp.concatenate([both[0:16], both[0:16], both[16:32]], axis=0)
                dist = jnp.dot(lhs, rhs, preferred_element_type=F32)
                inv = lax.rsqrt(dist)
                w_high, w_low = split2(inv * inv * inv)
                s = both[32:48]
                term = nt(s, w_high) + nt(s, w_low)
                total = term if total is None else total + term
            total = total[0:8] + total[8:16] + pltpu.roll(total[0:8], 4, 0)

            turned = picked[half].T
            lane_group = (cells_ref[pl.ds(group, 1), :] // 16) % 8
            feat = turned[0:16]
            for j in range(1, 8):
                feat = jnp.where(lane_group == j, turned[16 * j:16 * j + 16], feat)
            xyz = columns[pair, half * 64:half * 64 + 64, :]
            dx = xyz[:, 0:1] - feat[1:2]
            dy = xyz[:, 1:2] - feat[2:3]
            dz = xyz[:, 2:3] - feat[3:4]
            h = dx * dx + dy * dy + dz * dz + EPS
            inv = lax.rsqrt(h)
            inv2 = inv * inv
            inv3 = inv * inv2
            inv5 = inv3 * inv2
            qx = feat[4:5] * dx + feat[7:8] * dy + feat[8:9] * dz
            qy = feat[7:8] * dx + feat[5:6] * dy + feat[9:10] * dz
            qz = feat[8:9] * dx + feat[9:10] * dy + feat[6:7] * dz
            form = dx * qx + dy * qy + dz * qz
            along = feat[0:1] * inv3 + (2.5 * form) * (inv5 * inv2)
            pieces = []
            for d, q in ((dx, qx), (dy, qy), (dz, qz)):
                pieces.extend(split2(inv5 * q - along * d))
            far = nt(summing, jnp.concatenate(pieces, axis=1))
            here = total[0:3] - centre[:, half * 64:half * 64 + 64] * total[3:4]
            results.append(here + far[0:3])
        out_ref[:, pl.ds(pl.multiple_of(pair * 128, 128), 128)] = jnp.concatenate(results, axis=1)
        return 0

    lax.fori_loop(0, PAIRS, one_pair, 0)


def pull(positions, cell_list, leaf_list, leaves, table):
    vmem = pl.BlockSpec(memory_space=pltpu.VMEM)
    smem = pl.BlockSpec(memory_space=pltpu.SMEM)
    return pl.pallas_call(
        pull_kernel,
        name="pull",
        out_shape=jax.ShapeDtypeStruct((3, PAIRS * 128), F32),
        in_specs=[vmem, vmem, smem, vmem, vmem],
        out_specs=vmem,
        scratch_shapes=[
            pltpu.VMEM((2 * ALL_PAIRS, 48, 128), BF16),
            pltpu.VMEM((PAIRS, 128, 48), BF16),
            pltpu.VMEM((PAIRS, 128, 8), F32),
            pltpu.VMEM((128, 128), jnp.int32),
            pltpu.SMEM((128, 128), jnp.int32),
            pltpu.VMEM((2, 128, 128), F32),
            pltpu.SemaphoreType.DMA,
        ],
        compiler_params=pltpu.CompilerParams(vmem_limit_bytes=48 * 1024 * 1024),
    )(positions, cell_list, leaf_list, leaves, table)


def on_device(
    positions, masses, cell_mass, cell_center, cell_quad, cell_list, leaf_list, send_list, send_count,
):
    leaves, table = exchange(
        positions, masses.reshape(PAIRS, 128), cell_mass.reshape(1, 128), cell_center, cell_quad,
        send_list.reshape(2 * RANGE, CAP), send_count.reshape(2 * RANGE))
    return pull(positions, cell_list, leaf_list.T, leaves, table)


def solution(mesh):
    return jax.shard_map(
        on_device,
        mesh=mesh,
        in_specs=(
            P(None, ("dom", "sub")),
            P(("dom", "sub")),
            P(("dom", "sub")),
            P(None, ("dom", "sub")),
            P(None, ("dom", "sub")),
            P(("dom", "sub"), None),
            P(("dom", "sub"), None),
            P("dom", "sub", None, None),
            P("dom", "sub", None),
        ),
        out_specs=P(None, ("dom", "sub")),
        check_vma=False,
    )
```

time: 978 us -> 153 us (0.16)
  local copies, waits for them, and re-layouts: 774 us -> 7.46 us
  Pallas kernels: 0 us -> 145 us
  waiting for transfers between devices: 75.3 us -> 0 us
  other arithmetic: 72.5 us -> 0 us
  starting transfers between devices: 27 us -> 0 us
  between operations: 13.7 us -> 0.03 us
  blocking collectives: 10.8 us -> 0 us
    gather x66 -> x0, local copies, waits for them, and re-layouts: 746 us -> none  [the longest x32 592 us: group_pull(): picked = essential[:, particle_ids]]
    pallas_call x0 -> x2, Pallas kernels: none -> 145 us  [the longest x1 112 us: pull(): pl.pallas_call(pull_kernel, name='pull', out_shape=jax.ShapeDtypeStruct((...]
    all_gather x1 -> x0, waiting for transfers between devices: 75.3 us -> none  [on_device(): all_cells = lax.all_gather(cell_table, ('dom', 'sub'), axis=1, tiled=True)]
    reduce_sum x64 -> x0, other arithmetic: 38.1 us -> none  [the longest x16 14 us: direct_pull(): return jnp.sum(offset * factor[None], axis=-1)]
    ppermute x8 -> x0, starting transfers between devices: 27 us -> none  [passed_along(): lax.ppermute(value, axis, [(source, source + steps) for source in range(l...]
    while x2 -> x0, local copies, waits for them, and re-layouts: 19.5 us -> none  [on_device(): pulled = lax.map(one_block, (target_blocks, leaf_blocks, cell_blocks))]
    div x16 -> x0, other arithmetic: 12.2 us -> none  [direct_pull(): factor = weights[:, None, :] / (dist_sq * jnp.sqrt(dist_sq))]
    gather x33 -> x0, other arithmetic: 11.4 us -> none  [the longest x16 11.2 us: group_pull(): moments = cell_table[:, cell_ids]]
  transfers between devices with their start and end apart: 9 -> 0, of which waited for: 1 -> 0; matrix products, arithmetic and copies ran while one was open for 1% -> 0% of each run, Pallas kernels for 0% -> 0%
where the time goes in v1:
time: 153 us
  Pallas kernels  145 us (95%)
  local copies, waits for them, and re-layouts  7.46 us (5%)
    pallas_call x1, Pallas kernels, pull(): pl.pallas_call(pull_kernel, name='pull', out_shape=jax.ShapeDtypeStruct((...  112 us
    pallas_call x1, Pallas kernels, exchange(): pl.pallas_call(exchange_kernel, name='exchange', out_shape=(jax.ShapeDtyp...  33 us
    unnamed x20, local copies, waits for them, and re-layouts  7.46 us

profile of v1, /device:TPU:1, one launch (start us, length us, event | category | flops | bytes accessed | tf_op | source)
XLA Modules:
  0.0 152.7 jit_solution(13885504634599045310)
XLA Ops:
  0.0 0.0 copy-start
  0.0 0.9 copy-done
  0.9 0.0 copy-start.3
  0.9 0.8 copy-done.3
  1.7 0.0 copy-start.5
  1.7 0.7 copy-done.5
  2.4 0.0 copy-start.6
  2.4 0.7 copy-done.6
  3.0 0.0 copy-start.7
  3.0 0.7 copy-done.7
  3.7 0.0 copy-start.8
  3.7 0.7 copy-done.8
  4.4 0.0 copy-start.9
  4.4 0.7 copy-done.9
  5.0 33.0 %exchange.1 = (f32[288,4,128]{2,1,0:T(4,128)S(1)}, f32[4096,1,128]{2,1,0:T(1,128)S(1)}) custom-call(f32[3,8192]{1,0:T(4,128)S(1)} %copy-done, f32[64,128]{1,0:T(8,128)S(1)} %bitcast.5, f32[1,128]{1,0:T(1,128)S(1)} %bitcast.8, f32[3,128]{1,0:T(4,128)S(1)} %copy-done.7, f32[6,128]{1,0:T(8,128)S(1)} %copy-done.5, s32[8,8]{1,0:T(8,128)S(1)} %bitcast.7, s32[8]{0:T(128)S(1)} %bitcast.9), custom_call_target="tpu_custom_call" | custom-call | tf_op jit(solution)/shard_map/exchange/pallas_call | solution.py:187
  38.1 0.0 copy-start.1
  38.1 0.9 copy-done.1
  39.0 0.0 copy-start.2
  39.0 0.8 copy-done.2
  39.8 0.0 copy-start.4
  39.8 0.7 copy-done.4
  40.5 112.2 %pull.1 = f32[3,8192]{1,0:T(4,128)} custom-call(f32[3,8192]{1,0:T(4,128)S(1)} %copy-done.1, s32[128,128]{1,0:T(8,128)S(1)} %copy-done.2, s32[16,128]{1,0:T(8,128)S(1)} %bitcast.6, f32[288,4,128]{2,1,0:T(4,128)S(1)} %get-tuple-element.7.leaf_ref, f32[4096,1,128]{2,1,0:T(1,128)S(1)} %get-tuple-element.8.table_ref), custom_call_target="tpu_custom_call" | custom-call | tf_op jit(solution)/shard_map/pull/pallas_call | solution.py:356
Async XLA Ops:
  0.0 0.9 copy-start
  0.9 0.8 copy-start.3
  1.7 0.7 copy-start.5
  2.4 0.7 copy-start.6
  3.0 0.7 copy-start.7
  3.7 0.7 copy-start.8
  4.4 0.7 copy-start.9
  38.1 0.9 copy-start.1
  39.0 0.8 copy-start.2
  39.8 0.7 copy-start.4

commit v2 on v1

--- a/solution.py
+++ b/solution.py
@@ -243,7 +243,7 @@
 
 def pull_kernel(
     pos_ref, cells_ref, leaf_ids, leaf_ref, table_ref, out_ref,
-    sources, targets, columns, rows_vmem, rows_smem, picked, row_sem,
+    features, moments, targets, columns, rows_vmem, rows_smem, picked_a, picked_b, dist_a, dist_b, row_sem,
 ):
     rows_vmem[...] = cell_row(cells_ref[...])
     row_copy = pltpu.make_async_copy(rows_vmem, rows_smem, row_sem)
@@ -251,6 +251,7 @@
 
     row8 = lax.broadcasted_iota(jnp.int32, (8, 128), 0)
     one_row = jnp.where(row8 == 4, 1.0, 0.0).astype(F32)
+    no_rows = jnp.zeros((16, 128), F32)
 
     def prepare(pair, _):
         raw4 = leaf_ref[pair]
@@ -263,16 +264,19 @@
         s = jnp.where(row8 < 3, centred * mass, jnp.where(row8 == 3, mass, 0.0))
         u_high, u_mid, u_low = split3(u)
         s_high, s_mid, s_low = split3(s)
-        s_top = s_high + pltpu.roll(s_mid, 4, 0)
-        full = jnp.concatenate([u_high, u_mid, u_high, u_low, s_top, s_low], axis=0)
-        sources[2 * pair] = full.astype(BF16)
-        sources[2 * pair + 1] = pltpu.roll(full, LEAF, 1).astype(BF16)
+        s_full = jnp.concatenate([s_high + pltpu.roll(s_mid, 4, 0), s_low], axis=0)
+        moments[2 * pair] = s_full.astype(BF16)
+        moments[2 * pair + 1] = pltpu.roll(s_full, LEAF, 1).astype(BF16)
+        u_full = jnp.concatenate([u_high, u_mid, u_high, u_mid, u_high, u_low, no_rows], axis=0).astype(BF16)
+        turned = jnp.concatenate([u_full, u_full], axis=0).T
+        features[2 * pair] = turned[0:64]
+        features[2 * pair + 1] = turned[64:128]
         return 0
 
     lax.fori_loop(0, ALL_PAIRS, prepare, 0, unroll=4)
 
-    for pair in range(PAIRS):
-        raw3 = pos_ref[:, pair * 128:(pair + 1) * 128]
+    def prepare_targets(pair, _):
+        raw3 = pos_ref[:, pl.ds(pl.multiple_of(pair * 128, 128), 128)]
         raw = jnp.concatenate([raw3, jnp.zeros((5, 128), F32)], axis=0)
         centred = raw - 0.5
         square = jnp.where(row8 < 3, centred * centred, 0.0)
@@ -280,74 +284,123 @@
         t = jnp.where(row8 < 3, -2.0 * centred,
                       jnp.where(row8 == 3, 1.0, jnp.where(row8 == 4, norm, 0.0)))
         t_high, t_mid, t_low = split3(t)
-        full = jnp.concatenate(
-            [t_high, t_high, t_mid, t_mid, t_low, t_high, raw, jnp.zeros((128 - 56, 128), F32)], axis=0)
-        turned = full.T
-        targets[pair] = turned[:, 0:48].astype(BF16)
-        columns[pair] = turned[:, 48:56]
-
+        targets[pair] = jnp.concatenate(
+            [t_high, t_high, t_mid, t_mid, t_low, t_high, no_rows], axis=0).astype(BF16)
+        columns[pair] = jnp.concatenate([raw, jnp.zeros((120, 128), F32)], axis=0).T[:, 0:8]
+        return 0
+
+    lax.fori_loop(0, PAIRS, prepare_targets, 0, unroll=4)
     row_copy.wait()
 
-    low_half = lax.broadcasted_iota(jnp.int32, (48, 128), 1) < LEAF
+    low_half = lax.broadcasted_iota(jnp.int32, (64, 128), 1) < LEAF
+    low_half16 = lax.broadcasted_iota(jnp.int32, (16, 128), 1) < LEAF
     summing_row = lax.broadcasted_iota(jnp.int32, (8, 768), 0)
     summing_lane = lax.broadcasted_iota(jnp.int32, (8, 768), 1)
     summing = jnp.where(summing_row == (summing_lane // 256), 1.0, 0.0).astype(BF16)
-
-    def one_pair(pair, _):
-        results = []
-        centre = pos_ref[:, pl.ds(pl.multiple_of(pair * 128, 128), 128)] - 0.5
+    lane_block = lax.broadcasted_iota(jnp.int32, (8, 256), 1) // LEAF
+    nothing = jnp.zeros((64, 128), BF16)
+
+    def target_weights(quad):
+        blocks = []
         for half in range(2):
-            group = 2 * pair + half
-            for k in range(NCELL):
-                picked[half, k:k + 1, :] = table_ref[rows_smem[group, k]]
-            lhs = targets[pair, half * 64:half * 64 + 64, :]
-            total = None
-            for tile in range(4):
-                parts = []
-                for j in range(2):
-                    slot = 4 * tile + 2 * j
-                    low = leaf_ids[slot, group]
-                    high = leaf_ids[slot + 1, group]
-                    parts.append(jnp.where(low_half, sources[low], sources[high ^ 1]))
-                both = jnp.concatenate(parts, axis=1)
-                rhs = jnp.concatenate([both[0:16], both[0:16], both[16:32]], axis=0)
-                dist = jnp.dot(lhs, rhs, preferred_element_type=F32)
-                inv = lax.rsqrt(dist)
-                w_high, w_low = split2(inv * inv * inv)
-                s = both[32:48]
-                term = nt(s, w_high) + nt(s, w_low)
-                total = term if total is None else total + term
-            total = total[0:8] + total[8:16] + pltpu.roll(total[0:8], 4, 0)
-
-            turned = picked[half].T
-            lane_group = (cells_ref[pl.ds(group, 1), :] // 16) % 8
-            feat = turned[0:16]
-            for j in range(1, 8):
-                feat = jnp.where(lane_group == j, turned[16 * j:16 * j + 16], feat)
-            xyz = columns[pair, half * 64:half * 64 + 64, :]
-            dx = xyz[:, 0:1] - feat[1:2]
-            dy = xyz[:, 1:2] - feat[2:3]
-            dz = xyz[:, 2:3] - feat[3:4]
-            h = dx * dx + dy * dy + dz * dz + EPS
-            inv = lax.rsqrt(h)
-            inv2 = inv * inv
-            inv3 = inv * inv2
-            inv5 = inv3 * inv2
-            qx = feat[4:5] * dx + feat[7:8] * dy + feat[8:9] * dz
-            qy = feat[7:8] * dx + feat[5:6] * dy + feat[9:10] * dz
-            qz = feat[8:9] * dx + feat[9:10] * dy + feat[6:7] * dz
-            form = dx * qx + dy * qy + dz * qz
-            along = feat[0:1] * inv3 + (2.5 * form) * (inv5 * inv2)
-            pieces = []
-            for d, q in ((dx, qx), (dy, qy), (dz, qz)):
-                pieces.extend(split2(inv5 * q - along * d))
-            far = nt(summing, jnp.concatenate(pieces, axis=1))
-            here = total[0:3] - centre[:, half * 64:half * 64 + 64] * total[3:4]
-            results.append(here + far[0:3])
-        out_ref[:, pl.ds(pl.multiple_of(pair * 128, 128), 128)] = jnp.concatenate(results, axis=1)
+            tile = targets[2 * quad + half]
+            own = jnp.concatenate(
+                [jnp.where(low_half, tile, nothing), jnp.where(low_half, nothing, tile)], axis=0)
+            empty = jnp.zeros((128, 128), BF16)
+            blocks.append(jnp.concatenate([own, empty] if half == 0 else [empty, own], axis=0))
+        return jnp.concatenate(blocks, axis=1)
+
+    def fetch(quad, part, weights, picked, dist):
+        group = 4 * quad + part
+        for k in range(NCELL):
+            picked[part, k:k + 1, :] = table_ref[rows_smem[group, k]]
+        rows = []
+        for slot in range(4 * part, 4 * part + 4):
+            halves = []
+            for half in range(2):
+                first = leaf_ids[slot, 4 * quad + 2 * half]
+                second = leaf_ids[slot, 4 * quad + 2 * half + 1]
+                halves.append(jnp.where(low_half, features[first], features[second]))
+            rows.append(jnp.concatenate(halves, axis=1))
+        lhs = jnp.concatenate(rows, axis=0)
+        dist[part] = jnp.dot(lhs, weights, preferred_element_type=F32)
+
+    def weigh(quad, part, dist, totals):
+        inv = lax.rsqrt(dist[part])
+        w_high, w_low = split2(inv * inv * inv)
+        rows = []
+        for j in range(4):
+            group = 4 * quad + j
+            tiles = []
+            for slot in range(4 * part, 4 * part + 4, 2):
+                low = leaf_ids[slot, group]
+                high = leaf_ids[slot + 1, group]
+                tiles.append(jnp.where(low_half16, moments[low], moments[high ^ 1]))
+            rows.append(jnp.concatenate(tiles, axis=1))
+        full = jnp.concatenate(rows, axis=0)
+        short = jnp.concatenate([row[0:8] for row in rows], axis=0)
+        high = jnp.dot(full, w_high, preferred_element_type=F32)
+        low = jnp.dot(short, w_low, preferred_element_type=F32)
+        if totals is None:
+            return high, low
+        return totals[0] + high, totals[1] + low
+
+    def multipole(quad, part, picked):
+        group = 4 * quad + part
+        turned = picked[part].T
+        lane_group = (cells_ref[pl.ds(group, 1), :] // 16) % 8
+        feat = turned[0:16]
+        for j in range(1, 8):
+            feat = jnp.where(lane_group == j, turned[16 * j:16 * j + 16], feat)
+        xyz = columns[2 * quad + part // 2, (part % 2) * 64:(part % 2) * 64 + 64, :]
+        dx = xyz[:, 0:1] - feat[1:2]
+        dy = xyz[:, 1:2] - feat[2:3]
+        dz = xyz[:, 2:3] - feat[3:4]
+        h = dx * dx + dy * dy + dz * dz + EPS
+        inv = lax.rsqrt(h)
+        inv2 = inv * inv
+        inv3 = inv * inv2
+        inv5 = inv3 * inv2
+        qx = feat[4:5] * dx + feat[7:8] * dy + feat[8:9] * dz
+        qy = feat[7:8] * dx + feat[5:6] * dy + feat[9:10] * dz
+        qz = feat[8:9] * dx + feat[9:10] * dy + feat[6:7] * dz
+        form = dx * qx + dy * qy + dz * qz
+        along = feat[0:1] * inv3 + (2.5 * form) * (inv5 * inv2)
+        pieces = []
+        for d, q in ((dx, qx), (dy, qy), (dz, qz)):
+            pieces.extend(split2(inv5 * q - along * d))
+        return jnp.concatenate(pieces, axis=1)
+
+    def step(quad, picked, dist, later, later_picked, later_dist):
+        totals = None
+        pieces = []
+        weights = target_weights(later)
+        for part in range(4):
+            fetch(later, part, weights, later_picked, later_dist)
+            totals = weigh(quad, part, dist, totals)
+            pieces.append(multipole(quad, part, picked))
+        far = nt(summing, jnp.concatenate(pieces, axis=0))
+        high, low = totals
+        near = jnp.zeros((8, 256), F32)
+        for j in range(4):
+            block = high[16 * j:16 * j + 8] + high[16 * j + 8:16 * j + 16] + low[8 * j:8 * j + 8]
+            near = jnp.where(lane_block == j, block, near)
+        near = near + pltpu.roll(near, 4, 0)
+        lanes = pl.ds(pl.multiple_of(quad * 256, 256), 256)
+        centre = pos_ref[:, lanes] - 0.5
+        out_ref[:, lanes] = near[0:3] - centre * near[3:4] + far[0:3]
+
+    first_weights = target_weights(0)
+    for part in range(4):
+        fetch(0, part, first_weights, picked_a, dist_a)
+    quads = PAIRS // 2
+
+    def two_quads(i, _):
+        step(2 * i, picked_a, dist_a, 2 * i + 1, picked_b, dist_b)
+        step(2 * i + 1, picked_b, dist_b, jnp.minimum(2 * i + 2, quads - 1), picked_a, dist_a)
         return 0
 
-    lax.fori_loop(0, PAIRS, one_pair, 0)
+    lax.fori_loop(0, quads // 2, two_quads, 0)
 
 
 def pull(positions, cell_list, leaf_list, leaves, table):
@@ -360,12 +413,16 @@
         in_specs=[vmem, vmem, smem, vmem, vmem],
         out_specs=vmem,
         scratch_shapes=[
-            pltpu.VMEM((2 * ALL_PAIRS, 48, 128), BF16),
-            pltpu.VMEM((PAIRS, 128, 48), BF16),
+            pltpu.VMEM((2 * ALL_PAIRS, 64, 128), BF16),
+            pltpu.VMEM((2 * ALL_PAIRS, 16, 128), BF16),
+            pltpu.VMEM((PAIRS, 64, 128), BF16),
             pltpu.VMEM((PAIRS, 128, 8), F32),
             pltpu.VMEM((128, 128), jnp.int32),
             pltpu.SMEM((128, 128), jnp.int32),
-            pltpu.VMEM((2, 128, 128), F32),
+            pltpu.VMEM((4, 128, 128), F32),
+            pltpu.VMEM((4, 128, 128), F32),
+            pltpu.VMEM((4, 256, 256), F32),
+            pltpu.VMEM((4, 256, 256), F32),
             pltpu.SemaphoreType.DMA,
         ],
         compiler_params=pltpu.CompilerParams(vmem_limit_bytes=48 * 1024 * 1024),

time: 153 us -> 85.8 us (0.56)
  Pallas kernels: 145 us -> 78 us
    pallas_call x1, Pallas kernels: 112 us -> 45 us  [pull(): pl.pallas_call(pull_kernel, name='pull', out_shape=jax.ShapeDtypeStruct((...]
where the time goes in v2:
time: 85.8 us; the launch traced here: 85.5 us
  Pallas kernels  78 us (91%)
  local copies, waits for them, and re-layouts  7.46 us (9%)
    pallas_call x1, Pallas kernels, pull(): pl.pallas_call(pull_kernel, name='pull', out_shape=jax.ShapeDtypeStruct((...  45 us
    pallas_call x1, Pallas kernels, exchange(): pl.pallas_call(exchange_kernel, name='exchange', out_shape=(jax.ShapeDtyp...  33 us
    unnamed x20, local copies, waits for them, and re-layouts  7.46 us

profile of v2, /device:TPU:1, one launch (start us, length us, event | category | flops | bytes accessed | tf_op | source)
XLA Modules:
  0.0 85.5 jit_solution(6823492694040407805)
XLA Ops:
  0.0 0.0 copy-start
  0.0 0.9 %copy-done = f32[3,8192]{1,0:T(4,128)S(1)} copy-done((f32[3,8192]{1,0:T(4,128)S(1)}, f32[3,8192]{1,0:T(4,128)}, u32[]{:S(2)}) %copy-start) | copy-done | bytes 98328
  0.9 0.0 copy-start.3
  0.9 0.8 copy-done.3
  1.7 0.0 copy-start.5
  1.7 0.7 copy-done.5
  2.4 0.0 copy-start.6
  2.4 0.7 copy-done.6
  3.0 0.0 copy-start.7
  3.0 0.7 copy-done.7
  3.7 0.0 copy-start.8
  3.7 0.7 copy-done.8
  4.4 0.0 copy-start.9
  4.4 0.7 copy-done.9
  5.0 33.0 %exchange.1 = (f32[288,4,128]{2,1,0:T(4,128)S(1)}, f32[4096,1,128]{2,1,0:T(1,128)S(1)}) custom-call(f32[3,8192]{1,0:T(4,128)S(1)} %copy-done, f32[64,128]{1,0:T(8,128)S(1)} %bitcast.5, f32[1,128]{1,0:T(1,128)S(1)} %bitcast.8, f32[3,128]{1,0:T(4,128)S(1)} %copy-done.7, f32[6,128]{1,0:T(8,128)S(1)} %copy-done.5, s32[8,8]{1,0:T(8,128)S(1)} %bitcast.7, s32[8]{0:T(128)S(1)} %bitcast.9), custom_call_target="tpu_custom_call" | custom-call | tf_op jit(solution)/shard_map/exchange/pallas_call | solution.py:187
  38.1 0.0 copy-start.1
  38.1 0.9 %copy-done.1 = f32[3,8192]{1,0:T(4,128)S(1)} copy-done((f32[3,8192]{1,0:T(4,128)S(1)}, f32[3,8192]{1,0:T(4,128)}, u32[]{:S(2)}) %copy-start.1) | copy-done | bytes 98328
  39.0 0.0 copy-start.2
  39.0 0.8 copy-done.2
  39.8 0.0 copy-start.4
  39.8 0.7 copy-done.4
  40.5 45.0 %pull.1 = f32[3,8192]{1,0:T(4,128)} custom-call(f32[3,8192]{1,0:T(4,128)S(1)} %copy-done.1, s32[128,128]{1,0:T(8,128)S(1)} %copy-done.2, s32[16,128]{1,0:T(8,128)S(1)} %bitcast.6, f32[288,4,128]{2,1,0:T(4,128)S(1)} %get-tuple-element.7.leaf_ref, f32[4096,1,128]{2,1,0:T(1,128)S(1)} %get-tuple-element.8.table_ref), custom_call_target="tpu_custom_call" | custom-call | tf_op jit(solution)/shard_map/pull/pallas_call | solution.py:409
Async XLA Ops:
  0.0 0.9 %copy-start = (f32[3,8192]{1,0:T(4,128)S(1)}, f32[3,8192]{1,0:T(4,128)}, u32[]{:S(2)}) copy-start(f32[3,8192]{1,0:T(4,128)} %pos_ref.3) | copy-start | bytes 294916
  0.9 0.8 copy-start.3
  1.7 0.7 copy-start.5
  2.4 0.7 copy-start.6
  3.0 0.7 copy-start.7
  3.7 0.7 copy-start.8
  4.4 0.7 copy-start.9
  38.1 0.9 %copy-start.1 = (f32[3,8192]{1,0:T(4,128)S(1)}, f32[3,8192]{1,0:T(4,128)}, u32[]{:S(2)}) copy-start(f32[3,8192]{1,0:T(4,128)} %pos_ref.3) | copy-start | bytes 294916
  39.0 0.8 copy-start.2
  39.8 0.7 copy-start.4

commit v3 on v2

v3 whole, which is shorter than its diff:
```python
import functools

import jax
import jax.numpy as jnp
from jax import lax
from jax.experimental import pallas as pl
from jax.experimental.pallas import tpu as pltpu
from jax.sharding import PartitionSpec as P

LEAF = 64
NCELL = 128
NLEAF = 16
RANGE = 4
CAP = 8
EPS = 0.0025
F32 = jnp.float32
BF16 = jnp.bfloat16
MESH = pl.DeviceIdType.MESH

NX, NY, NZ, NCORE = 4, 4, 8, 2
SIZES = {"x": NX, "y": NY, "z": NZ}
ROWS = 16
PARTS = ((0, 8, ("z", "x", "y")), (8, 8, ("z", "y", "x")))
OFFSETS = tuple(range(-RANGE, 0)) + tuple(range(1, RANGE + 1))
PAIRS = 64
ALL_PAIRS = NY * PAIRS + len(OFFSETS) * CAP // 2
N_CELL_ROWS = NX * NY * NZ * NCORE * ROWS
STAGE_AT = ((0, 1), (8, 2))


def split3(value):
    high = value.astype(BF16).astype(F32)
    rest = value - high
    mid = rest.astype(BF16).astype(F32)
    return high, mid, rest - mid


def split2(value):
    high = value.astype(BF16)
    return high, (value - high.astype(F32)).astype(BF16)


def nt(a, b):
    return lax.dot_general(a, b, (((1,), (1,)), ((), ())), preferred_element_type=F32)


def cell_row(cell):
    shard = cell // 128
    sub = shard % NY
    dom = shard // NY
    at = {"x": dom // (NZ * NCORE), "z": (dom // NCORE) % NZ, "y": sub}
    core = dom % NCORE
    row = cell % 16
    n = N_CELL_ROWS // ROWS
    result = None
    for first, rows, order in PARTS:
        index, stride = 0, 1
        for axis in order:
            index = index + at[axis] * stride
            stride = stride * SIZES[axis]
        index = index + core * stride
        here = n * first + index * rows + (row - first)
        result = here if result is None else jnp.where(row >= first, here, result)
    return result


def kernel(
    pos_hbm, mass_hbm, cmass_hbm, ccen_hbm, cquad_hbm, cells_hbm, leaf_hbm, list_hbm, count_hbm,
    out_ref,
    pos_ref, mass_ref, cmass_ref, ccen_ref, cquad_ref, cells_ref, leaf_ids, send_list, send_count,
    pad, own, far_out, leaf_ref, table_ref,
    features, moments, targets, columns, rows_vmem, rows_smem, picked_a, picked_b, dist_a, dist_b,
    load_sem, row_sem, near_send, near_recv, far_send, far_recv, cell_send, cell_recv, core_send, core_recv,
):
    dom = lax.axis_index("dom")
    sub = lax.axis_index("sub")
    core = dom % NCORE
    at = {"x": dom // (NZ * NCORE), "z": (dom // NCORE) % NZ, "y": sub}
    n_dom = NX * NZ * NCORE
    base = sub * PAIRS

    loads = [
        pltpu.make_async_copy(src, dst, load_sem.at[i])
        for i, (src, dst) in enumerate((
            (pos_hbm, pos_ref), (mass_hbm, mass_ref), (cmass_hbm, cmass_ref), (ccen_hbm, ccen_ref),
            (cquad_hbm, cquad_ref), (list_hbm, send_list), (count_hbm, send_count), (cells_hbm, cells_ref),
            (leaf_hbm, leaf_ids)))
    ]
    for load in loads:
        load.start()

    def device(x, y, z, c):
        return ((x * NZ + z) * NCORE + c, y)

    def peer(axis, step):
        where = dict(at)
        where[axis] = (at[axis] + step) % SIZES[axis]
        return device(where["x"], where["y"], where["z"], core)

    barrier = pltpu.get_barrier_semaphore()
    waits = 0
    for axis in ("x", "y", "z"):
        for step in range(1, SIZES[axis]):
            pl.semaphore_signal(barrier, inc=1, device_id=peer(axis, step), device_id_type=MESH)
            waits += 1
    other_core = device(at["x"], at["y"], at["z"], 1 - core)
    pl.semaphore_signal(barrier, inc=1, device_id=other_core, device_id_type=MESH)
    waits += 1
    for off in OFFSETS:
        pl.semaphore_signal(barrier, inc=1, device_id=((dom + off + n_dom) % n_dom, sub), device_id_type=MESH)
        waits += 1

    for load in loads[0:5]:
        load.wait()
    for j in range(PAIRS):
        own[j, 0:3, :] = pos_ref[:, j * 128:(j + 1) * 128]
        own[j, 3:4, :] = mass_ref[j:j + 1, :]
    pad[...] = jnp.zeros((128, 128), F32)
    pad[0:1, :] = cmass_ref[...]
    pad[1:4, :] = ccen_ref[...]
    pad[4:10, :] = cquad_ref[...]
    by_cell = pad[...].T
    packed = by_cell[0:16, :]
    for g in range(1, 8):
        packed = packed + pltpu.roll(by_cell[16 * g:16 * g + 16, :], 16 * g, 1)
    pad[0:16, :] = packed

    def start_of(part, done):
        first, rows, order = PARTS[part]
        size = rows
        n = N_CELL_ROWS // ROWS
        index = 0
        stride = 1
        for s, axis in enumerate(order):
            if s >= done:
                index = index + at[axis] * stride
            stride = stride * SIZES[axis]
        index = index + core * stride
        for axis in order[:done]:
            size = size * SIZES[axis]
        return n * first + index * rows, size

    for part, (first, rows, order) in enumerate(PARTS):
        start, _ = start_of(part, 0)
        for r in range(rows):
            table_ref[start + r, :, :] = pad[first + r:first + r + 1, :]

    pl.semaphore_wait(barrier, waits)

    def cell_copy(part, stage, step):
        axis = PARTS[part][2][stage]
        start, size = start_of(part, stage)
        block = table_ref.at[pl.ds(start, size)]
        return pltpu.make_async_remote_copy(
            src_ref=block, dst_ref=block,
            send_sem=cell_send.at[part, stage, step], recv_sem=cell_recv.at[part, stage, step],
            device_id=peer(axis, step), device_id_type=MESH)

    def stage_copies(part, stage):
        return [cell_copy(part, stage, step) for step in range(1, SIZES[PARTS[part][2][stage]])]

    def core_copy(part):
        start, size = start_of(part, 3)
        block = table_ref.at[pl.ds(start, size)]
        return pltpu.make_async_remote_copy(
            src_ref=block, dst_ref=block, send_sem=core_send.at[part], recv_sem=core_recv.at[part],
            device_id=other_core, device_id_type=MESH)

    n_parts = len(PARTS)

    def start_stage(stage):
        for part in range(n_parts):
            if stage == 3:
                core_copy(part).start()
            else:
                for copy in stage_copies(part, stage):
                    copy.start()

    def finish_stage(stage):
        for part in range(n_parts):
            if stage == 3:
                core_copy(part).wait_recv()
            else:
                for copy in stage_copies(part, stage):
                    copy.wait_recv()

    near = [
        pltpu.make_async_remote_copy(
            src_ref=own, dst_ref=leaf_ref.at[pl.ds(base, PAIRS)],
            send_sem=near_send.at[step], recv_sem=near_recv.at[step],
            device_id=peer("y", step), device_id_type=MESH)
        for step in range(1, NY)
    ]
    for copy in near:
        copy.start()
    start_stage(0)

    for load in loads[5:7]:
        load.wait()
    low_half4 = lax.broadcasted_iota(jnp.int32, (4, 128), 1) < LEAF

    def far_pair(slot, t):
        halves = []
        for h in range(2):
            block = send_list[slot, 2 * t + h]
            tile = own[block // 2]
            turned = pltpu.roll(tile, LEAF, 1)
            picked = jnp.where(block % 2 == h, tile, turned)
            inside = jnp.logical_and(dom + OFFSETS[slot] >= 0, dom + OFFSETS[slot] < n_dom)
            live = jnp.logical_and(inside, 2 * t + h < send_count[slot])
            halves.append(jnp.where(live, picked, jnp.zeros_like(picked)))
        far_out[slot, t] = jnp.where(low_half4, halves[0], halves[1])

    def far_copy(slot):
        return pltpu.make_async_remote_copy(
            src_ref=far_out.at[slot],
            dst_ref=leaf_ref.at[pl.ds(NY * PAIRS + slot * (CAP // 2), CAP // 2)],
            send_sem=far_send.at[slot], recv_sem=far_recv.at[slot],
            device_id=((dom + OFFSETS[slot] + n_dom) % n_dom, sub), device_id_type=MESH)

    for slot in range(len(OFFSETS)):
        for t in range(CAP // 2):
            far_pair(slot, t)
    far = [far_copy(slot) for slot in range(len(OFFSETS))]
    for copy in far:
        copy.start()

    for load in loads[7:9]:
        load.wait()
    rows_vmem[...] = cell_row(cells_ref[...])
    row_copy = pltpu.make_async_copy(rows_vmem, rows_smem, row_sem)
    row_copy.start()

    row8 = lax.broadcasted_iota(jnp.int32, (8, 128), 0)
    one_row = jnp.where(row8 == 4, 1.0, 0.0).astype(F32)
    no_rows = jnp.zeros((16, 128), F32)

    def prepare(source_ref, source, pair):
        raw4 = source_ref[source]
        raw = jnp.concatenate([raw4, raw4], axis=0)
        mass = raw4[3:4, :]
        centred = raw - 0.5
        square = jnp.where(row8 < 3, centred * centred, 0.0)
        norm = jnp.sum(square, axis=0, keepdims=True) + EPS
        u = jnp.where(row8 < 3, centred, jnp.where(row8 == 3, norm, one_row))
        s = jnp.where(row8 < 3, centred * mass, jnp.where(row8 == 3, mass, 0.0))
        u_high, u_mid, u_low = split3(u)
        s_high, s_mid, s_low = split3(s)
        s_full = jnp.concatenate([s_high + pltpu.roll(s_mid, 4, 0), s_low], axis=0)
        moments[2 * pair] = s_full.astype(BF16)
        moments[2 * pair + 1] = pltpu.roll(s_full, LEAF, 1).astype(BF16)
        u_full = jnp.concatenate([u_high, u_mid, u_high, u_mid, u_high, u_low, no_rows], axis=0).astype(BF16)
        turned = jnp.concatenate([u_full, u_full], axis=0).T
        features[2 * pair] = turned[0:64]
        features[2 * pair + 1] = turned[64:128]

    def prepare_range(source_ref, source, pair, count):
        def body(j, _):
            prepare(source_ref, source + j, pair + j)
            return 0
        lax.fori_loop(0, count, body, 0, unroll=4)

    def prepare_targets(pair, _):
        raw3 = pos_ref[:, pl.ds(pl.multiple_of(pair * 128, 128), 128)]
        raw = jnp.concatenate([raw3, jnp.zeros((5, 128), F32)], axis=0)
        centred = raw - 0.5
        square = jnp.where(row8 < 3, centred * centred, 0.0)
        norm = jnp.sum(square, axis=0, keepdims=True)
        t = jnp.where(row8 < 3, -2.0 * centred,
                      jnp.where(row8 == 3, 1.0, jnp.where(row8 == 4, norm, 0.0)))
        t_high, t_mid, t_low = split3(t)
        targets[pair] = jnp.concatenate(
            [t_high, t_high, t_mid, t_mid, t_low, t_high, no_rows], axis=0).astype(BF16)
        columns[pair] = jnp.concatenate([raw, jnp.zeros((120, 128), F32)], axis=0).T[:, 0:8]
        return 0

    prepare_range(own, 0, base, PAIRS)
    lax.fori_loop(0, PAIRS, prepare_targets, 0, unroll=4)
    finish_stage(0)
    start_stage(1)
    for copy in far:
        copy.wait_recv()
    prepare_range(leaf_ref, NY * PAIRS, NY * PAIRS, len(OFFSETS) * CAP // 2)
    for step in range(1, NY):
        near[step - 1].wait_recv()
        origin = ((sub + NY - step) % NY) * PAIRS
        prepare_range(leaf_ref, origin, origin, PAIRS)

    low_half = lax.broadcasted_iota(jnp.int32, (64, 128), 1) < LEAF
    low_half16 = lax.broadcasted_iota(jnp.int32, (16, 128), 1) < LEAF
    summing_row = lax.broadcasted_iota(jnp.int32, (8, 768), 0)
    summing_lane = lax.broadcasted_iota(jnp.int32, (8, 768), 1)
    summing = jnp.where(summing_row == (summing_lane // 256), 1.0, 0.0).astype(BF16)
    lane_block = lax.broadcasted_iota(jnp.int32, (8, 256), 1) // LEAF
    nothing = jnp.zeros((64, 128), BF16)
    empty = jnp.zeros((128, 128), BF16)

    def target_weights(quad):
        blocks = []
        for half in range(2):
            tile = targets[2 * quad + half]
            diagonal = jnp.concatenate(
                [jnp.where(low_half, tile, nothing), jnp.where(low_half, nothing, tile)], axis=0)
            blocks.append(jnp.concatenate([diagonal, empty] if half == 0 else [empty, diagonal], axis=0))
        return jnp.concatenate(blocks, axis=1)

    def distances(quad, part, weights, dist):
        rows = []
        for slot in range(4 * part, 4 * part + 4):
            halves = []
            for half in range(2):
                first = leaf_ids[slot, 4 * quad + 2 * half]
                second = leaf_ids[slot, 4 * quad + 2 * half + 1]
                halves.append(jnp.where(low_half, features[first], features[second]))
            rows.append(jnp.concatenate(halves, axis=1))
        lhs = jnp.concatenate(rows, axis=0)
        dist[part] = jnp.dot(lhs, weights, preferred_element_type=F32)

    def weigh(quad, part, dist, totals):
        inv = lax.rsqrt(dist[part])
        w_high, w_low = split2(inv * inv * inv)
        rows = []
        for j in range(4):
            group = 4 * quad + j
            tiles = []
            for slot in range(4 * part, 4 * part + 4, 2):
                low = leaf_ids[slot, group]
                high = leaf_ids[slot + 1, group]
                tiles.append(jnp.where(low_half16, moments[low], moments[high ^ 1]))
            rows.append(jnp.concatenate(tiles, axis=1))
        full = jnp.concatenate(rows, axis=0)
        short = jnp.concatenate([row[0:8] for row in rows], axis=0)
        high = jnp.dot(full, w_high, preferred_element_type=F32)
        low = jnp.dot(short, w_low, preferred_element_type=F32)
        if totals is None:
            return high, low
        return totals[0] + high, totals[1] + low

    def quad_lanes(quad):
        return pl.ds(pl.multiple_of(quad * 256, 256), 256)

    def direct(quad, dist, later, later_dist):
        totals = None
        weights = target_weights(later)
        for part in range(4):
            distances(later, part, weights, later_dist)
            totals = weigh(quad, part, dist, totals)
        high, low = totals
        near_sum = jnp.zeros((8, 256), F32)
        for j in range(4):
            block = high[16 * j:16 * j + 8] + high[16 * j + 8:16 * j + 16] + low[8 * j:8 * j + 8]
            near_sum = jnp.where(lane_block == j, block, near_sum)
        near_sum = near_sum + pltpu.roll(near_sum, 4, 0)
        lanes = quad_lanes(quad)
        centre = pos_ref[:, lanes] - 0.5
        out_ref[:, lanes] = near_sum[0:3] - centre * near_sum[3:4]

    def gather(quad, part, picked):
        group = 4 * quad + part
        for k in range(NCELL):
            picked[part, k:k + 1, :] = table_ref[rows_smem[group, k]]

    def multipole(quad, part, picked):
        group = 4 * quad + part
        turned = picked[part].T
        lane_group = (cells_ref[pl.ds(group, 1), :] // 16) % 8
        feat = turned[0:16]
        for j in range(1, 8):
            feat = jnp.where(lane_group == j, turned[16 * j:16 * j + 16], feat)
        xyz = columns[2 * quad + part // 2, (part % 2) * 64:(part % 2) * 64 + 64, :]
        dx = xyz[:, 0:1] - feat[1:2]
        dy = xyz[:, 1:2] - feat[2:3]
        dz = xyz[:, 2:3] - feat[3:4]
        h = dx * dx + dy * dy + dz * dz + EPS
        inv = lax.rsqrt(h)
        inv2 = inv * inv
        inv3 = inv * inv2
        inv5 = inv3 * inv2
        qx = feat[4:5] * dx + feat[7:8] * dy + feat[8:9] * dz
        qy = feat[7:8] * dx + feat[5:6] * dy + feat[9:10] * dz
        qz = feat[8:9] * dx + feat[9:10] * dy + feat[6:7] * dz
        form = dx * qx + dy * qy + dz * qz
        along = feat[0:1] * inv3 + (2.5 * form) * (inv5 * inv2)
        pieces = []
        for d, q in ((dx, qx), (dy, qy), (dz, qz)):
            pieces.extend(split2(inv5 * q - along * d))
        return jnp.concatenate(pieces, axis=1)

    def cells_pull(quad, picked, later, later_picked):
        pieces = []
        for part in range(4):
            gather(later, part, later_picked)
            pieces.append(multipole(quad, part, picked))
        far_sum = nt(summing, jnp.concatenate(pieces, axis=0))
        lanes = quad_lanes(quad)
        out_ref[:, lanes] = out_ref[:, lanes] + far_sum[0:3]

    quads = PAIRS // 2
    first_weights = target_weights(0)
    for part in range(4):
        distances(0, part, first_weights, dist_a)

    def direct_two(i, _):
        for when, stage in STAGE_AT:
            @pl.when(i == when)
            def _():
                finish_stage(stage)
                start_stage(stage + 1)
        direct(2 * i, dist_a, 2 * i + 1, dist_b)
        direct(2 * i + 1, dist_b, jnp.minimum(2 * i + 2, quads - 1), dist_a)
        return 0

    lax.fori_loop(0, quads // 2, direct_two, 0)
    row_copy.wait()
    finish_stage(3)
    for part in range(4):
        gather(0, part, picked_a)

    def cells_two(i, _):
        cells_pull(2 * i, picked_a, 2 * i + 1, picked_b)
        cells_pull(2 * i + 1, picked_b, jnp.minimum(2 * i + 2, quads - 1), picked_a)
        return 0

    lax.fori_loop(0, quads // 2, cells_two, 0)

    for copy in near + far:
        copy.wait_send()
    for stage in range(3):
        for part in range(n_parts):
            for copy in stage_copies(part, stage):
                copy.wait_send()
    for part in range(n_parts):
        core_copy(part).wait_send()


def on_device(
    positions, masses, cell_mass, cell_center, cell_quad, cell_list, leaf_list, send_list, send_count,
):
    dma = pltpu.SemaphoreType.DMA
    n_off = len(OFFSETS)
    n_parts = len(PARTS)
    return pl.pallas_call(
        kernel,
        name="tree_pull",
        out_shape=jax.ShapeDtypeStruct((3, PAIRS * 128), F32),
        in_specs=[pl.BlockSpec(memory_space=pl.ANY)] * 9,
        out_specs=pl.BlockSpec(memory_space=pltpu.VMEM),
        scratch_shapes=[
            pltpu.VMEM((3, PAIRS * 128), F32),
            pltpu.VMEM((PAIRS, 128), F32),
            pltpu.VMEM((1, 128), F32),
            pltpu.VMEM((3, 128), F32),
            pltpu.VMEM((6, 128), F32),
            pltpu.VMEM((128, 128), jnp.int32),
            pltpu.SMEM((NLEAF, 128), jnp.int32),
            pltpu.SMEM((n_off, CAP), jnp.int32),
            pltpu.SMEM((n_off,), jnp.int32),
            pltpu.VMEM((128, 128), F32),
            pltpu.VMEM((PAIRS, 4, 128), F32),
            pltpu.VMEM((n_off, CAP // 2, 4, 128), F32),
            pltpu.VMEM((ALL_PAIRS, 4, 128), F32),
            pltpu.VMEM((N_CELL_ROWS, 1, 128), F32),
            pltpu.VMEM((2 * ALL_PAIRS, 64, 128), BF16),
            pltpu.VMEM((2 * ALL_PAIRS, 16, 128), BF16),
            pltpu.VMEM((PAIRS, 64, 128), BF16),
            pltpu.VMEM((PAIRS, 128, 8), F32),
            pltpu.VMEM((128, 128), jnp.int32),
            pltpu.SMEM((128, 128), jnp.int32),
            pltpu.VMEM((4, 128, 128), F32),
            pltpu.VMEM((4, 128, 128), F32),
            pltpu.VMEM((4, 256, 256), F32),
            pltpu.VMEM((4, 256, 256), F32),
            dma((9,)), dma,
            dma((NY,)), dma((NY,)), dma((n_off,)), dma((n_off,)),
            dma((n_parts, 3, NZ)), dma((n_parts, 3, NZ)), dma((n_parts,)), dma((n_parts,)),
        ],
        compiler_params=pltpu.CompilerParams(
            collective_id=0, has_side_effects=True, vmem_limit_bytes=60 * 1024 * 1024),
    )(
        positions, masses.reshape(PAIRS, 128), cell_mass.reshape(1, 128), cell_center, cell_quad,
        cell_list, leaf_list.T, send_list.reshape(2 * RANGE, CAP), send_count.reshape(2 * RANGE))


def solution(mesh):
    return jax.shard_map(
        on_device,
        mesh=mesh,
        in_specs=(
            P(None, ("dom", "sub")),
            P(("dom", "sub")),
            P(("dom", "sub")),
            P(None, ("dom", "sub")),
            P(None, ("dom", "sub")),
            P(("dom", "sub"), None),
            P(("dom", "sub"), None),
            P("dom", "sub", None, None),
            P("dom", "sub", None),
        ),
        out_specs=P(None, ("dom", "sub")),
        check_vma=False,
    )
```

time: 85.8 us -> 68.8 us (0.80)
  Pallas kernels: 78 us -> 67.1 us
  local copies, waits for them, and re-layouts: 7.46 us -> 1.58 us
    pallas_call x2 -> x1, Pallas kernels: 78 us -> 67.1 us  [on_device(): pl.pallas_call(kernel, name='tree_pull', out_shape=jax.ShapeDtypeStruct((...]
    unnamed x20 -> x1, local copies, waits for them, and re-layouts: 7.46 us -> 1.58 us
where the time goes in v3:
time: 68.8 us; the launch traced here: 68.7 us
  Pallas kernels  67.1 us (98%)
  local copies, waits for them, and re-layouts  1.58 us (2%)
    pallas_call x1, Pallas kernels, on_device(): pl.pallas_call(kernel, name='tree_pull', out_shape=jax.ShapeDtypeStruct((...  67.1 us
    unnamed x1, local copies, waits for them, and re-layouts  1.58 us

profile of v3, /device:TPU:1, one launch (start us, length us, event | category | flops | bytes accessed | tf_op | source)
XLA Modules:
  0.0 68.7 jit_solution(15921333239047843912)
XLA Ops:
  0.0 67.1 %tree_pull.1 = f32[3,8192]{1,0:T(4,128)} custom-call(f32[3,8192]{1,0:T(4,128)} %pos_hbm.1, f32[64,128]{1,0:T(8,128)} %bitcast.5, f32[1,128]{1,0:T(1,128)} %bitcast.8, f32[3,128]{1,0:T(4,128)} %ccen_hbm.1, f32[6,128]{1,0:T(8,128)} %cquad_hbm.1, s32[128,128]{1,0:T(8,128)} %cells_hbm.1, s32[16,128]{1,0:T(8,128)} %bitcast.6, s32[8,8]{1,0:T(8,128)} %bitcast.7, ...), custom_call_target="tpu_custom_call" | custom-call | tf_op jit(solution)/shard_map/tree_pull/pallas_call | solution.py:442
  67.1 1.6 %copy.11 = f32[3,8192]{1,0:T(4,128)} copy(f32[3,8192]{1,0:T(4,128)} %tree_pull.1) | data formatting | bytes 196608

commit v4 on v3

--- a/solution.py
+++ b/solution.py
@@ -25,6 +25,8 @@
 PAIRS = 64
 ALL_PAIRS = NY * PAIRS + len(OFFSETS) * CAP // 2
 N_CELL_ROWS = NX * NY * NZ * NCORE * ROWS
+N_SLOTS = 8
+CHUNK = 16
 STAGE_AT = ((0, 1), (8, 2))
 
 
@@ -69,7 +71,8 @@
     out_ref,
     pos_ref, mass_ref, cmass_ref, ccen_ref, cquad_ref, cells_ref, leaf_ids, send_list, send_count,
     pad, own, far_out, leaf_ref, table_ref,
-    features, moments, targets, columns, rows_vmem, rows_smem, picked_a, picked_b, dist_a, dist_b,
+    features, moments, targets, columns, rows_vmem, rows_smem, picked_a, picked_b, feat_a, feat_b, pieces_a, pieces_b,
+    dist_a, dist_b,
     load_sem, row_sem, near_send, near_recv, far_send, far_recv, cell_send, cell_recv, core_send, core_recv,
 ):
     dom = lax.axis_index("dom")
@@ -144,92 +147,6 @@
         start, _ = start_of(part, 0)
         for r in range(rows):
             table_ref[start + r, :, :] = pad[first + r:first + r + 1, :]
-
-    pl.semaphore_wait(barrier, waits)
-
-    def cell_copy(part, stage, step):
-        axis = PARTS[part][2][stage]
-        start, size = start_of(part, stage)
-        block = table_ref.at[pl.ds(start, size)]
-        return pltpu.make_async_remote_copy(
-            src_ref=block, dst_ref=block,
-            send_sem=cell_send.at[part, stage, step], recv_sem=cell_recv.at[part, stage, step],
-            device_id=peer(axis, step), device_id_type=MESH)
-
-    def stage_copies(part, stage):
-        return [cell_copy(part, stage, step) for step in range(1, SIZES[PARTS[part][2][stage]])]
-
-    def core_copy(part):
-        start, size = start_of(part, 3)
-        block = table_ref.at[pl.ds(start, size)]
-        return pltpu.make_async_remote_copy(
-            src_ref=block, dst_ref=block, send_sem=core_send.at[part], recv_sem=core_recv.at[part],
-            device_id=other_core, device_id_type=MESH)
-
-    n_parts = len(PARTS)
-
-    def start_stage(stage):
-        for part in range(n_parts):
-            if stage == 3:
-                core_copy(part).start()
-            else:
-                for copy in stage_copies(part, stage):
-                    copy.start()
-
-    def finish_stage(stage):
-        for part in range(n_parts):
-            if stage == 3:
-                core_copy(part).wait_recv()
-            else:
-                for copy in stage_copies(part, stage):
-                    copy.wait_recv()
-
-    near = [
-        pltpu.make_async_remote_copy(
-            src_ref=own, dst_ref=leaf_ref.at[pl.ds(base, PAIRS)],
-            send_sem=near_send.at[step], recv_sem=near_recv.at[step],
-            device_id=peer("y", step), device_id_type=MESH)
-        for step in range(1, NY)
-    ]
-    for copy in near:
-        copy.start()
-    start_stage(0)
-
-    for load in loads[5:7]:
-        load.wait()
-    low_half4 = lax.broadcasted_iota(jnp.int32, (4, 128), 1) < LEAF
-
-    def far_pair(slot, t):
-        halves = []
-        for h in range(2):
-            block = send_list[slot, 2 * t + h]
-            tile = own[block // 2]
-            turned = pltpu.roll(tile, LEAF, 1)
-            picked = jnp.where(block % 2 == h, tile, turned)
-            inside = jnp.logical_and(dom + OFFSETS[slot] >= 0, dom + OFFSETS[slot] < n_dom)
-            live = jnp.logical_and(inside, 2 * t + h < send_count[slot])
-            halves.append(jnp.where(live, picked, jnp.zeros_like(picked)))
-        far_out[slot, t] = jnp.where(low_half4, halves[0], halves[1])
-
-    def far_copy(slot):
-        return pltpu.make_async_remote_copy(
-            src_ref=far_out.at[slot],
-            dst_ref=leaf_ref.at[pl.ds(NY * PAIRS + slot * (CAP // 2), CAP // 2)],
-            send_sem=far_send.at[slot], recv_sem=far_recv.at[slot],
-            device_id=((dom + OFFSETS[slot] + n_dom) % n_dom, sub), device_id_type=MESH)
-
-    for slot in range(len(OFFSETS)):
-        for t in range(CAP // 2):
-            far_pair(slot, t)
-    far = [far_copy(slot) for slot in range(len(OFFSETS))]
-    for copy in far:
-        copy.start()
-
-    for load in loads[7:9]:
-        load.wait()
-    rows_vmem[...] = cell_row(cells_ref[...])
-    row_copy = pltpu.make_async_copy(rows_vmem, rows_smem, row_sem)
-    row_copy.start()
 
     row8 = lax.broadcasted_iota(jnp.int32, (8, 128), 0)
     one_row = jnp.where(row8 == 4, 1.0, 0.0).astype(F32)
@@ -258,7 +175,7 @@
         def body(j, _):
             prepare(source_ref, source + j, pair + j)
             return 0
-        lax.fori_loop(0, count, body, 0, unroll=4)
+        lax.fori_loop(0, count, body, 0, unroll=8)
 
     def prepare_targets(pair, _):
         raw3 = pos_ref[:, pl.ds(pl.multiple_of(pair * 128, 128), 128)]
@@ -275,7 +192,102 @@
         return 0
 
     prepare_range(own, 0, base, PAIRS)
-    lax.fori_loop(0, PAIRS, prepare_targets, 0, unroll=4)
+    lax.fori_loop(0, PAIRS, prepare_targets, 0, unroll=8)
+    for load in loads[7:9]:
+        load.wait()
+    cells = cells_ref[...]
+    found = cell_row(cells)
+    for quad in range(PAIRS // 2):
+        rows_vmem[quad] = found[4 * quad:4 * quad + 4]
+    cells_ref[...] = (cells >> 4) & 7
+
+    def row_copy(quad, slot):
+        return pltpu.make_async_copy(rows_vmem.at[quad], rows_smem[slot], row_sem.at[slot])
+
+    row_copy(0, N_SLOTS - 1).start()
+    for slot in range(N_SLOTS - 1):
+        row_copy(slot + 1, slot).start()
+
+    pl.semaphore_wait(barrier, waits)
+
+    def cell_copy(part, stage, step):
+        axis = PARTS[part][2][stage]
+        start, size = start_of(part, stage)
+        block = table_ref.at[pl.ds(start, size)]
+        return pltpu.make_async_remote_copy(
+            src_ref=block, dst_ref=block,
+            send_sem=cell_send.at[part, stage, step], recv_sem=cell_recv.at[part, stage, step],
+            device_id=peer(axis, step), device_id_type=MESH)
+
+    def stage_copies(part, stage):
+        return [cell_copy(part, stage, step) for step in range(1, SIZES[PARTS[part][2][stage]])]
+
+    def core_copy(part):
+        start, size = start_of(part, 3)
+        block = table_ref.at[pl.ds(start, size)]
+        return pltpu.make_async_remote_copy(
+            src_ref=block, dst_ref=block, send_sem=core_send.at[part], recv_sem=core_recv.at[part],
+            device_id=other_core, device_id_type=MESH)
+
+    n_parts = len(PARTS)
+
+    def start_stage(stage):
+        for part in range(n_parts):
+            if stage == 3:
+                core_copy(part).start()
+            else:
+                for copy in stage_copies(part, stage):
+                    copy.start()
+
+    def finish_stage(stage):
+        for part in range(n_parts):
+            if stage == 3:
+                core_copy(part).wait_recv()
+            else:
+                for copy in stage_copies(part, stage):
+                    copy.wait_recv()
+
+    near = [
+        pltpu.make_async_remote_copy(
+            src_ref=own, dst_ref=leaf_ref.at[pl.ds(base, PAIRS)],
+            send_sem=near_send.at[step], recv_sem=near_recv.at[step],
+            device_id=peer("y", step), device_id_type=MESH)
+        for step in range(1, NY)
+    ]
+    for copy in near:
+        copy.start()
+    start_stage(0)
+
+    for load in loads[5:7]:
+        load.wait()
+    low_half4 = lax.broadcasted_iota(jnp.int32, (4, 128), 1) < LEAF
+
+    def far_pair(slot, t):
+        halves = []
+        for h in range(2):
+            block = send_list[slot, 2 * t + h]
+            tile = own[block // 2]
+            turned = pltpu.roll(tile, LEAF, 1)
+            picked = jnp.where(block % 2 == h, tile, turned)
+            inside = jnp.logical_and(dom + OFFSETS[slot] >= 0, dom + OFFSETS[slot] < n_dom)
+            live = jnp.logical_and(inside, 2 * t + h < send_count[slot])
+            halves.append(jnp.where(live, picked, jnp.zeros_like(picked)))
+        far_out[slot, t] = jnp.where(low_half4, halves[0], halves[1])
+
+    def far_copy(slot):
+        return pltpu.make_async_remote_copy(
+            src_ref=far_out.at[slot],
+            dst_ref=leaf_ref.at[pl.ds(NY * PAIRS + slot * (CAP // 2), CAP // 2)],
+            send_sem=far_send.at[slot], recv_sem=far_recv.at[slot],
+            device_id=((dom + OFFSETS[slot] + n_dom) % n_dom, sub), device_id_type=MESH)
+
+    for slot in range(len(OFFSETS)):
+        for t in range(CAP // 2):
+            far_pair(slot, t)
+    far = [far_copy(slot) for slot in range(len(OFFSETS))]
+    for copy in far:
+        copy.start()
+
     finish_stage(0)
     start_stage(1)
     for copy in far:
@@ -355,45 +367,57 @@
         centre = pos_ref[:, lanes] - 0.5
         out_ref[:, lanes] = near_sum[0:3] - centre * near_sum[3:4]
 
-    def gather(quad, part, picked):
-        group = 4 * quad + part
-        for k in range(NCELL):
-            picked[part, k:k + 1, :] = table_ref[rows_smem[group, k]]
-
-    def multipole(quad, part, picked):
-        group = 4 * quad + part
+    def gather(slot, part, start, count, picked):
+        rows = rows_smem[slot]
+        for k in range(start, start + count):
+            row = table_ref[rows[part, k]]
+            picked[part, k:k + 1, :] = row
+        return row
+
+    def cell_features(quad, part, picked, feat_ref):
         turned = picked[part].T
-        lane_group = (cells_ref[pl.ds(group, 1), :] // 16) % 8
+        lane_group = cells_ref[pl.ds(4 * quad + part, 1), :]
         feat = turned[0:16]
         for j in range(1, 8):
             feat = jnp.where(lane_group == j, turned[16 * j:16 * j + 16], feat)
-        xyz = columns[2 * quad + part // 2, (part % 2) * 64:(part % 2) * 64 + 64, :]
-        dx = xyz[:, 0:1] - feat[1:2]
-        dy = xyz[:, 1:2] - feat[2:3]
-        dz = xyz[:, 2:3] - feat[3:4]
+        feat_ref[part] = feat
+
+    def multipole(quad, part, start, feat_ref, pieces, after):
+        first = (part % 2) * 64 + start
+        xyz = columns[2 * quad + part // 2, first:first + CHUNK, :]
+        feat = [feat_ref[part, f:f + 1, :] for f in range(10)]
+        if after is not None:
+            feat[9] = feat[9] + after * 0.0
+        dx = xyz[:, 0:1] - feat[1]
+        dy = xyz[:, 1:2] - feat[2]
+        dz = xyz[:, 2:3] - feat[3]
         h = dx * dx + dy * dy + dz * dz + EPS
         inv = lax.rsqrt(h)
         inv2 = inv * inv
-        inv3 = inv * inv2
-        inv5 = inv3 * inv2
-        qx = feat[4:5] * dx + feat[7:8] * dy + feat[8:9] * dz
-        qy = feat[7:8] * dx + feat[5:6] * dy + feat[9:10] * dz
-        qz = feat[8:9] * dx + feat[9:10] * dy + feat[6:7] * dz
+        inv5 = inv2 * inv2 * inv
+        qx = feat[4] * dx + feat[7] * dy + feat[8] * dz
+        qy = feat[7] * dx + feat[5] * dy + feat[9] * dz
+        qz = feat[8] * dx + feat[9] * dy + feat[6] * dz
         form = dx * qx + dy * qy + dz * qz
-        along = feat[0:1] * inv3 + (2.5 * form) * (inv5 * inv2)
-        pieces = []
-        for d, q in ((dx, qx), (dy, qy), (dz, qz)):
-            pieces.extend(split2(inv5 * q - along * d))
-        return jnp.concatenate(pieces, axis=1)
-
-    def cells_pull(quad, picked, later, later_picked):
-        pieces = []
+        along = feat[0] * h + (2.5 * form) * inv2
+        row = part * 64 + start
+        for c, (d, q) in enumerate(((dx, qx), (dy, qy), (dz, qz))):
+            high, low = split2(inv5 * (q - along * d))
+            pieces[row:row + CHUNK, 256 * c:256 * c + 128] = high
+            pieces[row:row + CHUNK, 256 * c + 128:256 * c + 256] = low
+
+    def cells_pull(quad, feat_ref, pieces, later, slot, later_picked, later_feat, after):
+        steps = LEAF // CHUNK
         for part in range(4):
-            gather(later, part, later_picked)
-            pieces.append(multipole(quad, part, picked))
-        far_sum = nt(summing, jnp.concatenate(pieces, axis=0))
+            for c in range(steps):
+                fetched = gather(slot, part, c * (NCELL // steps), NCELL // steps, later_picked)
+                multipole(quad, part, c * CHUNK, feat_ref, pieces, after)
+                after = fetched
+            cell_features(later, part, later_picked, later_feat)
+        far_sum = nt(summing, pieces[...])
         lanes = quad_lanes(quad)
         out_ref[:, lanes] = out_ref[:, lanes] + far_sum[0:3]
+        return after
 
     quads = PAIRS // 2
     first_weights = target_weights(0)
@@ -411,17 +435,32 @@
         return 0
 
     lax.fori_loop(0, quads // 2, direct_two, 0)
-    row_copy.wait()
     finish_stage(3)
+    row_copy(0, N_SLOTS - 1).wait()
     for part in range(4):
-        gather(0, part, picked_a)
-
-    def cells_two(i, _):
-        cells_pull(2 * i, picked_a, 2 * i + 1, picked_b)
-        cells_pull(2 * i + 1, picked_b, jnp.minimum(2 * i + 2, quads - 1), picked_a)
+        gather(N_SLOTS - 1, part, 0, NCELL, picked_a)
+        cell_features(0, part, picked_a, feat_a)
+    row_copy(N_SLOTS, N_SLOTS - 1).start()
+
+    def cells_some(i, _):
+        for block in range(0, N_SLOTS, 4):
+            for slot in range(block, block + 4):
+                row_copy(0, slot).wait()
+            after = None
+            for slot in range(block, block + 4):
+                quad = N_SLOTS * i + slot
+                later = jnp.minimum(quad + 1, quads - 1)
+                if slot % 2 == 0:
+                    after = cells_pull(quad, feat_a, pieces_a, later, slot, picked_b, feat_b, after)
+                else:
+                    after = cells_pull(quad, feat_b, pieces_b, later, slot, picked_a, feat_a, after)
+            for slot in range(block, block + 4):
+                row_copy(jnp.minimum(N_SLOTS * (i + 1) + slot + 1, quads - 1), slot).start()
         return 0
 
-    lax.fori_loop(0, quads // 2, cells_two, 0)
+    lax.fori_loop(0, quads // N_SLOTS, cells_some, 0)
+    for slot in range(N_SLOTS):
+        row_copy(0, slot).wait()
 
     for copy in near + far:
         copy.wait_send()
@@ -464,13 +503,17 @@
             pltpu.VMEM((2 * ALL_PAIRS, 16, 128), BF16),
             pltpu.VMEM((PAIRS, 64, 128), BF16),
             pltpu.VMEM((PAIRS, 128, 8), F32),
-            pltpu.VMEM((128, 128), jnp.int32),
-            pltpu.SMEM((128, 128), jnp.int32),
+            pltpu.VMEM((PAIRS // 2, 4, 128), jnp.int32),
+            [pltpu.SMEM((4, 128), jnp.int32) for _ in range(N_SLOTS)],
             pltpu.VMEM((4, 128, 128), F32),
             pltpu.VMEM((4, 128, 128), F32),
+            pltpu.VMEM((4, 16, 128), F32),
+            pltpu.VMEM((4, 16, 128), F32),
+            pltpu.VMEM((256, 768), BF16),
+            pltpu.VMEM((256, 768), BF16),
             pltpu.VMEM((4, 256, 256), F32),
             pltpu.VMEM((4, 256, 256), F32),
-            dma((9,)), dma,
+            dma((9,)), dma((N_SLOTS,)),
             dma((NY,)), dma((NY,)), dma((n_off,)), dma((n_off,)),
             dma((n_parts, 3, NZ)), dma((n_parts, 3, NZ)), dma((n_parts,)), dma((n_parts,)),
         ],

time: 68.8 us -> 63.1 us (0.917)
  Pallas kernels: 67.1 us -> 61.4 us
    pallas_call x1, Pallas kernels: 67.1 us -> 61.4 us  [on_device(): pl.pallas_call(kernel, name='tree_pull', out_shape=jax.ShapeDtypeStruct((...]
where the time goes in v4:
time: 63.1 us; the launch traced here: 63 us
  Pallas kernels  61.4 us (97%)
  local copies, waits for them, and re-layouts  1.58 us (3%)
    pallas_call x1, Pallas kernels, on_device(): pl.pallas_call(kernel, name='tree_pull', out_shape=jax.ShapeDtypeStruct((...  61.4 us
    unnamed x1, local copies, waits for them, and re-layouts  1.58 us

profile of v4, /device:TPU:1, one launch (start us, length us, event | category | flops | bytes accessed | tf_op | source)
XLA Modules:
  0.0 63.0 jit_solution(1579649856148989987)
XLA Ops:
  0.0 61.4 %tree_pull.1 = f32[3,8192]{1,0:T(4,128)} custom-call(f32[3,8192]{1,0:T(4,128)} %pos_hbm.1, f32[64,128]{1,0:T(8,128)} %bitcast.5, f32[1,128]{1,0:T(1,128)} %bitcast.8, f32[3,128]{1,0:T(4,128)} %ccen_hbm.1, f32[6,128]{1,0:T(8,128)} %cquad_hbm.1, s32[128,128]{1,0:T(8,128)} %cells_hbm.1, s32[16,128]{1,0:T(8,128)} %bitcast.6, s32[8,8]{1,0:T(8,128)} %bitcast.7, ...), custom_call_target="tpu_custom_call" | custom-call | tf_op jit(solution)/shard_map/tree_pull/pallas_call | solution.py:481
  61.4 1.6 %copy.11 = f32[3,8192]{1,0:T(4,128)} copy(f32[3,8192]{1,0:T(4,128)} %tree_pull.1) | data formatting | bytes 196608

commit v5 on v4

--- a/solution.py
+++ b/solution.py
@@ -26,8 +26,9 @@
 ALL_PAIRS = NY * PAIRS + len(OFFSETS) * CAP // 2
 N_CELL_ROWS = NX * NY * NZ * NCORE * ROWS
 N_SLOTS = 8
-CHUNK = 16
-STAGE_AT = ((0, 1), (8, 2))
+LAG = 2
+CHUNK = 32
+STAGE_AT = ((0, 1), (4, 2))
 
 
 def split3(value):
@@ -367,10 +368,12 @@
         centre = pos_ref[:, lanes] - 0.5
         out_ref[:, lanes] = near_sum[0:3] - centre * near_sum[3:4]
 
-    def gather(slot, part, start, count, picked):
+    def gather(slot, part, start, count, picked, after=None):
         rows = rows_smem[slot]
         for k in range(start, start + count):
             row = table_ref[rows[part, k]]
+            if after is not None and k == start + count - 1:
+                row = row + after * 0.0
             picked[part, k:k + 1, :] = row
         return row
 
@@ -405,36 +408,41 @@
             high, low = split2(inv5 * (q - along * d))
             pieces[row:row + CHUNK, 256 * c:256 * c + 128] = high
             pieces[row:row + CHUNK, 256 * c + 128:256 * c + 256] = low
+        return inv5[0:1] * along[0:1]
 
     def cells_pull(quad, feat_ref, pieces, later, slot, later_picked, later_feat, after):
         steps = LEAF // CHUNK
+        fetched, summed = after
         for part in range(4):
             for c in range(steps):
-                fetched = gather(slot, part, c * (NCELL // steps), NCELL // steps, later_picked)
-                multipole(quad, part, c * CHUNK, feat_ref, pieces, after)
-                after = fetched
+                back = summed[-LAG] if len(summed) >= LAG else None
+                row = gather(slot, part, c * (NCELL // steps), NCELL // steps, later_picked, back)
+                summed = summed + [multipole(quad, part, c * CHUNK, feat_ref, pieces, fetched)]
+                fetched = row
             cell_features(later, part, later_picked, later_feat)
         far_sum = nt(summing, pieces[...])
         lanes = quad_lanes(quad)
         out_ref[:, lanes] = out_ref[:, lanes] + far_sum[0:3]
-        return after
+        return fetched, summed
 
     quads = PAIRS // 2
     first_weights = target_weights(0)
     for part in range(4):
         distances(0, part, first_weights, dist_a)
 
-    def direct_two(i, _):
+    def direct_four(i, _):
         for when, stage in STAGE_AT:
             @pl.when(i == when)
             def _():
                 finish_stage(stage)
                 start_stage(stage + 1)
-        direct(2 * i, dist_a, 2 * i + 1, dist_b)
-        direct(2 * i + 1, dist_b, jnp.minimum(2 * i + 2, quads - 1), dist_a)
+        for j in range(0, 4, 2):
+            quad = 4 * i + j
+            direct(quad, dist_a, quad + 1, dist_b)
+            direct(quad + 1, dist_b, jnp.minimum(quad + 2, quads - 1), dist_a)
         return 0
 
-    lax.fori_loop(0, quads // 2, direct_two, 0)
+    lax.fori_loop(0, quads // 4, direct_four, 0)
     finish_stage(3)
     row_copy(0, N_SLOTS - 1).wait()
     for part in range(4):
@@ -446,7 +454,7 @@
         for block in range(0, N_SLOTS, 4):
             for slot in range(block, block + 4):
                 row_copy(0, slot).wait()
-            after = None
+            after = (None, [])
             for slot in range(block, block + 4):
                 quad = N_SLOTS * i + slot
                 later = jnp.minimum(quad + 1, quads - 1)

time: 63.1 us -> 60 us (0.951)
  Pallas kernels: 61.4 us -> 58.3 us
    pallas_call x1, Pallas kernels: 61.4 us -> 58.3 us  [on_device(): pl.pallas_call(kernel, name='tree_pull', out_shape=jax.ShapeDtypeStruct((...]
where the time goes in v5:
time: 60 us; the launch traced here: 59.9 us
  Pallas kernels  58.3 us (97%)
  local copies, waits for them, and re-layouts  1.58 us (3%)
    pallas_call x1, Pallas kernels, on_device(): pl.pallas_call(kernel, name='tree_pull', out_shape=jax.ShapeDtypeStruct((...  58.3 us
    unnamed x1, local copies, waits for them, and re-layouts  1.58 us

profile of v5, /device:TPU:1, one launch (start us, length us, event | category | flops | bytes accessed | tf_op | source)
XLA Modules:
  0.0 59.9 jit_solution(7362543920403201077)
XLA Ops:
  0.0 58.3 %tree_pull.1 = f32[3,8192]{1,0:T(4,128)} custom-call(f32[3,8192]{1,0:T(4,128)} %pos_hbm.1, f32[64,128]{1,0:T(8,128)} %bitcast.5, f32[1,128]{1,0:T(1,128)} %bitcast.8, f32[3,128]{1,0:T(4,128)} %ccen_hbm.1, f32[6,128]{1,0:T(8,128)} %cquad_hbm.1, s32[128,128]{1,0:T(8,128)} %cells_hbm.1, s32[16,128]{1,0:T(8,128)} %bitcast.6, s32[8,8]{1,0:T(8,128)} %bitcast.7, ...), custom_call_target="tpu_custom_call" | custom-call | tf_op jit(solution)/shard_map/tree_pull/pallas_call | solution.py:489
  58.3 1.6 %copy.11 = f32[3,8192]{1,0:T(4,128)} copy(f32[3,8192]{1,0:T(4,128)} %tree_pull.1) | data formatting | bytes 196608

commit v6 on v5

--- a/solution.py
+++ b/solution.py
@@ -28,7 +28,7 @@
 N_SLOTS = 8
 LAG = 2
 CHUNK = 32
-STAGE_AT = ((0, 1), (4, 2))
+STAGE_AT = ((4, 2),)
 
 
 def split3(value):
@@ -176,7 +176,7 @@
         def body(j, _):
             prepare(source_ref, source + j, pair + j)
             return 0
-        lax.fori_loop(0, count, body, 0, unroll=8)
+        lax.fori_loop(0, count, body, 0, unroll=16)
 
     def prepare_targets(pair, _):
         raw3 = pos_ref[:, pl.ds(pl.multiple_of(pair * 128, 128), 128)]
@@ -296,6 +296,9 @@
     prepare_range(leaf_ref, NY * PAIRS, NY * PAIRS, len(OFFSETS) * CAP // 2)
     for step in range(1, NY):
         near[step - 1].wait_recv()
+        if step == NY - 1:
+            finish_stage(1)
+            start_stage(2)
         origin = ((sub + NY - step) % NY) * PAIRS
         prepare_range(leaf_ref, origin, origin, PAIRS)
 

time: 60 us -> 58.8 us (0.980)
  Pallas kernels: 58.3 us -> 57.1 us
    pallas_call x1, Pallas kernels: 58.3 us -> 57.1 us  [on_device(): pl.pallas_call(kernel, name='tree_pull', out_shape=jax.ShapeDtypeStruct((...]
where the time goes in v6:
time: 58.8 us; the launch traced here: 58.7 us
  Pallas kernels  57.1 us (97%)
  local copies, waits for them, and re-layouts  1.58 us (3%)
    pallas_call x1, Pallas kernels, on_device(): pl.pallas_call(kernel, name='tree_pull', out_shape=jax.ShapeDtypeStruct((...  57.1 us
    unnamed x1, local copies, waits for them, and re-layouts  1.58 us

profile of v6, /device:TPU:1, one launch (start us, length us, event | category | flops | bytes accessed | tf_op | source)
XLA Modules:
  0.0 58.7 jit_solution(14639860247905179528)
XLA Ops:
  0.0 57.1 %tree_pull.1 = f32[3,8192]{1,0:T(4,128)} custom-call(f32[3,8192]{1,0:T(4,128)} %pos_hbm.1, f32[64,128]{1,0:T(8,128)} %bitcast.5, f32[1,128]{1,0:T(1,128)} %bitcast.8, f32[3,128]{1,0:T(4,128)} %ccen_hbm.1, f32[6,128]{1,0:T(8,128)} %cquad_hbm.1, s32[128,128]{1,0:T(8,128)} %cells_hbm.1, s32[16,128]{1,0:T(8,128)} %bitcast.6, s32[8,8]{1,0:T(8,128)} %bitcast.7, ...), custom_call_target="tpu_custom_call" | custom-call | tf_op jit(solution)/shard_map/tree_pull/pallas_call | solution.py:492
  57.1 1.6 %copy.11 = f32[3,8192]{1,0:T(4,128)} copy(f32[3,8192]{1,0:T(4,128)} %tree_pull.1) | data formatting | bytes 196608
